TPU v7x, 1024 devices: a whole 8x8x8 slice. The times are simulated.
1024 devices in a mesh: code: 64 (over x_hi, y, core), dp: 16 (over x_lo, z).
Axes of the slice: x: 8 (x_hi: 4, x_lo: 2; x = x_hi * 2 + x_lo), y: 8, z: 8, core: 2. Of those that a mesh axis runs over, the one named last changes fastest.
Arguments:
- cold_table: float32 [64, 16, 4, 512, 128], P('code', 'dp'), may hold values from -6 to 6
- block_ids: int32 [64, 16, 4], P('code', 'dp'), may hold values from 0 to 3
- counts: int32 [64, 16], P('code', 'dp'), may hold values from 1 to 4
- group_map: int32 [64], P('code'), may hold values from 0 to 7, as said below
- coef: float32 [2, 8], replicated, may hold values from 0.5 to 2
- batch_ids: int32 [64, 16, 1024], P('code', 'dp'), may hold values from 0 to 2047
- out_grad: float32 [64, 16, 1024, 128], P('code', 'dp'), may hold values from -6 to 6
- hot_weights: float32 [2048, 128], replicated, may hold values from -6 to 6
- accum: float32 [2048], replicated, may hold values from 0.01 to 1
Outputs:
- parity_shards: float32 [64, 16, 2, 4, 64, 128], P('code', 'dp')
- new_weights: float32 [2048, 128], replicated
- new_accum: float32 [2048], replicated
Inputs may be any that keep to these rules, and one draw needn't show every extreme that they name: `group_map`: each aligned run of 8 code positions holds each of 0 to 7 once.
All inputs are finite; a program needn't handle non-finite values.
Results may differ from a plain program's by a relative error of at most 0.0003.
Values sent between devices are 32-bit elements; how exact they have to be, the bound alone decides.
No kernel may reach another device: no remote copies, remote signals or barrier semaphores. Data moves between devices by JAX's collectives and lax.ppermute only.
A program may use at most 32 MiB of HBM per device.

v0:
```python
import jax
import jax.numpy as jnp
from jax import lax
from jax.sharding import PartitionSpec as P


def swapped(value, axis, apart):
    mask = 2**apart
    pairs = [(source, source ^ mask) for source in range(lax.axis_size(axis))]
    return lax.ppermute(value, axis, pairs)


def adagrad(grad, weights, accumulators):
    updated_accum = accumulators + jnp.mean(grad * grad, axis=1)
    updated = weights - 0.5 * grad / (jnp.sqrt(updated_accum)[:, None] + 1e-06)
    return (updated, updated_accum)


def shards(cold_table, block_ids, counts, group_map, coef, batch_ids, out_grad, hot_weights, accum):
    slot_count = block_ids.shape[2]
    block_rows = cold_table.shape[3]
    width = cold_table.shape[4]
    hot_rows = hot_weights.shape[0]
    part_rows = block_rows // 8
    selected = cold_table[0, 0][block_ids[0, 0]]
    live = (jnp.arange(slot_count) < counts[0, 0]).astype(jnp.float32)
    masked = selected * live[:, None, None]
    column = coef[:, group_map[0]]
    member = lax.axis_index("code") % 8
    summed = column[:, None, None, None] * masked[None]
    for bit_index in (0, 1, 2):
        summed = summed + swapped(summed, "code", bit_index)
    summed = summed.reshape(2, slot_count, 8, part_rows, width)
    owned = lax.dynamic_index_in_dim(summed, member, 2, keepdims=False)
    parity_shards = owned[None, None]
    onehot = (batch_ids[0, 0][:, None] == jnp.arange(hot_rows)[None, :]).astype(jnp.float32)
    local_grad = lax.dot_general(
        onehot,
        out_grad[0, 0],
        (((0,), (0,)), ((), ())),
        precision=lax.Precision.HIGHEST,
        preferred_element_type=jnp.float32,
    )
    grad = lax.psum(local_grad, ("code", "dp"))
    new_weights, new_accum = adagrad(grad, hot_weights, accum)
    return (parity_shards, new_weights, new_accum)


def solution(mesh):
    in_specs = (
        P("code", "dp", None, None, None),
        P("code", "dp", None),
        P("code", "dp"),
        P("code"),
        P(),
        P("code", "dp", None),
        P("code", "dp", None, None),
        P(),
        P(),
    )
    out_specs = (P("code", "dp", None, None, None, None), P(), P())
    return jax.shard_map(shards, mesh=mesh, in_specs=in_specs, out_specs=out_specs, check_vma=False)
```

profile of v0, /device:TPU:1, one launch (start us, length us, event | category | flops | bytes accessed | tf_op | source)
XLA Modules:
  0.0 420.9 jit_solution(11069476346564521091)
XLA Ops:
  7.2 0.0 copy-start
  7.2 0.0 all-reduce.2.cloned.1.call-start
  8.0 0.7 fusion.4
  9.3 0.9 dynamic-slice_reduce_fusion
  10.2 0.0 copy-done
  10.2 0.6 gather_fusion
  10.8 0.1 broadcast_multiply_fusion.1
  10.9 0.2 broadcast_multiply_fusion
  11.1 16.1 %collective-permute-start = (f32[2,4,512,128]{3,2,1,0:T(8,128)S(1)}, f32[2,4,512,128]{3,2,1,0:T(8,128)S(1)}, u32[]{:S(2)}, u32[]{:S(2)}) collective-permute-start(f32[2,4,512,128]{3,2,1,0:T(8,128)S(1)} %broadcast_multiply_fusion), channel_id=1, source_target_pairs={{0,16},{16,0},{32,48},{48,32},{64,80},{80,64},{96,112},{112,96},{1... | collective-permute-start | bytes 6291464 | tf_op jit(solution)/shard_map/ppermute | solution.py:10
  27.2 3.8 collective-permute-done
  31.0 0.2 fusion.3
  31.2 0.0 copy-start.2
  31.2 0.0 copy-start.3
  31.2 2.1 collective-permute-start.1
  33.3 46.8 %collective-permute-done.1 = f32[2,4,512,128]{3,2,1,0:T(8,128)S(1)} collective-permute-done((f32[2,4,512,128]{3,2,1,0:T(8,128)S(1)}, f32[2,4,512,128]{3,2,1,0:T(8,128)S(1)}, u32[]{:S(2)}, u32[]{:S(2)}) %collective-permute-start.1) | collective-permute-done | bytes 2097184 | tf_op jit(solution)/shard_map/ppermute | solution.py:10
  80.1 0.3 fusion.5
  80.4 1.9 collective-permute-start.2
  82.4 0.0 copy-done.2
  82.4 0.0 copy-done.3
  82.4 7.8 %fusion = f32[2048,128]{1,0:T(8,128)} fusion(s32[1024]{0:T(1024)S(1)} %bitcast.20, f32[1,1,1024,128]{3,2,1,0:T(8,128)S(1)} %copy-done.2), kind=kOutput, calls=%fused_computation.2 | convolution fusion | flops 3223322624 | bytes 1576960 | tf_op jit(solution)/shard_map/dot_general | solution.py:37
  90.2 0.0 copy-start.1
  90.2 0.0 all-reduce.2.cloned.1.call-update
  90.3 316.2 %all-reduce.2.cloned.1.call-done = f32[2048,128]{1,0:T(8,128)} async-done(((f32[2048,128]{1,0:T(8,128)}), f32[2048,128]{1,0:T(8,128)}) %all-reduce.2.cloned.1.call-update) | async-done | bytes 1048592 | tf_op jit(solution)/shard_map/psum | solution.py:44
  406.5 1.6 multiply_reduce_fusion
  408.1 0.0 copy-done.1
  408.1 0.6 sqrt_add_fusion
  408.7 2.9 divide_subtract_fusion
  411.5 0.0 collective-permute-done.2
  411.5 1.8 add.46
  413.3 0.7 dynamic-slice_bitcast_fusion
  (2 shorter events, 0.0 us)
Async XLA Ops:
  7.2 3.0 copy-start
  7.2 399.3 %all-reduce.2.cloned.1.call-start = ((), (), s32[]{:S(2)}) async-start(), calls=%async_computation | async-start | bytes 2097152 | tf_op jit(solution)/shard_map/psum | solution.py:44
  11.1 19.8 %collective-permute-start = (f32[2,4,512,128]{3,2,1,0:T(8,128)S(1)}, f32[2,4,512,128]{3,2,1,0:T(8,128)S(1)}, u32[]{:S(2)}, u32[]{:S(2)}) collective-permute-start(f32[2,4,512,128]{3,2,1,0:T(8,128)S(1)} %broadcast_multiply_fusion), channel_id=1, source_target_pairs={{0,16},{16,0},{32,48},{48,32},{64,80},{80,64},{96,112},{112,96},{1... | collective-permute-start | bytes 6291464 | tf_op jit(solution)/shard_map/ppermute | solution.py:10
  31.2 51.1 %copy-start.2 = (f32[1,1,1024,128]{3,2,1,0:T(8,128)S(1)}, f32[1,1,1024,128]{3,2,1,0:T(8,128)}, u32[]{:S(2)}) copy-start(f32[1,1,1024,128]{3,2,1,0:T(8,128)} %param.15) | copy-start | bytes 1572868
  31.2 51.1 %copy-start.3 = (s32[1,1,1024]{2,1,0:T(1,128)S(1)}, s32[1,1,1024]{2,1,0:T(1,128)}, u32[]{:S(2)}) copy-start(s32[1,1,1024]{2,1,0:T(1,128)} %param.14) | copy-start | bytes 12292
  31.2 48.9 %collective-permute-start.1 = (f32[2,4,512,128]{3,2,1,0:T(8,128)S(1)}, f32[2,4,512,128]{3,2,1,0:T(8,128)S(1)}, u32[]{:S(2)}, u32[]{:S(2)}) collective-permute-start(f32[2,4,512,128]{3,2,1,0:T(8,128)S(1)} %fusion.3), channel_id=1, source_target_pairs={{0,32},{16,48},{32,0},{48,16},{64,96},{80,112},{96,64},{112,80},{1... | collective-permute-start | bytes 6291464 | tf_op jit(solution)/shard_map/ppermute | solution.py:10
  80.4 331.1 %collective-permute-start.2 = (f32[2,4,512,128]{3,2,1,0:T(8,128)S(1)}, f32[2,4,512,128]{3,2,1,0:T(8,128)}, u32[]{:S(2)}, u32[]{:S(2)}) collective-permute-start(f32[2,4,512,128]{3,2,1,0:T(8,128)S(1)} %fusion.5), channel_id=1, source_target_pairs={{0,64},{16,80},{32,96},{48,112},{64,0},{80,16},{96,32},{112,48},{1... | collective-permute-start | bytes 6291464 | tf_op jit(solution)/shard_map/ppermute | solution.py:10
  90.2 317.8 %copy-start.1 = (f32[2048]{0:T(1024)S(1)}, f32[2048]{0:T(1024)}, u32[]{:S(2)}) copy-start(f32[2048]{0:T(1024)} %param.17) | copy-start | bytes 24580
Sparse Core Ops, SparseCore 0:
  90.4 316.0 all-reduce.1
where the time goes:
time: 421 us
  waiting for transfers between devices  367 us (87%)
  starting transfers between devices  20.1 us (5%)
  between operations  15.6 us (4%)
  other arithmetic  8.39 us (2%)
  matrix products  7.83 us (2%)
    psum x1, waiting for transfers between devices, shards(): grad = lax.psum(local_grad, ('code', 'dp'))  316 us
    ppermute x3, waiting for transfers between devices, swapped(): return lax.ppermute(value, axis, pairs)  50.6 us
    ppermute x3, starting transfers between devices, swapped(): return lax.ppermute(value, axis, pairs)  20 us
  transfers between devices with their start and end apart: 4, of which 3 were waited for; matrix products, arithmetic and copies ran while one was open for 3% of the time, Pallas kernels for 0%

commit v1 on v0

v1 whole, which is shorter than its diff:
```python
import jax
import jax.numpy as jnp
from jax import lax
from jax.sharding import Mesh, PartitionSpec as P

NAMES = ("xh", "xm", "yh", "ym", "yl", "core", "xl", "z")
SIZES = (2, 2, 2, 2, 2, 2, 2, 8)
CODE = ("xh", "xm", "yh", "ym", "yl", "core")
DP = ("xl", "z")
NEAR = ("xm", "xl", "z")
FAR = ("xh", "yh", "ym", "yl")


def size(axes):
    return lax.axis_size(axes)


def exchange(parts, axes):
    return lax.all_to_all(parts, axes, 0, 0, tiled=True)


def to_all(block, axes):
    return exchange(jnp.broadcast_to(block[None], (size(axes),) + block.shape), axes)


def swap(value, axis):
    return lax.ppermute(value, axis, [(0, 1), (1, 0)])


def pick(value, place, axis):
    return lax.dynamic_index_in_dim(value, place, axis, keepdims=False)


def adagrad(grad, weights, accumulators):
    updated_accum = accumulators + jnp.mean(grad * grad, axis=1)
    updated = weights - 0.5 * grad / (jnp.sqrt(updated_accum)[:, None] + 1e-06)
    return (updated, updated_accum)


def partial_grad(ids, rows_grad, first, rows):
    onehot = (ids[:, None] - first == jnp.arange(rows)[None, :]).astype(jnp.float32)
    return lax.dot_general(
        onehot,
        rows_grad,
        (((0,), (0,)), ((), ())),
        precision=lax.Precision.HIGHEST,
        preferred_element_type=jnp.float32,
    )


def shards(cold_table, block_ids, counts, group_map, coef, batch_ids, out_grad, hot_weights, accum):
    slot_count = block_ids.shape[2]
    block_rows = cold_table.shape[3]
    width = cold_table.shape[4]
    hot_rows = hot_weights.shape[0]
    part_rows = block_rows // 8
    core = lax.axis_index("core")

    live = (jnp.arange(slot_count) < counts[0, 0]).astype(jnp.float32)
    masked = cold_table[0, 0][block_ids[0, 0]] * live[:, None, None]
    column = coef[:, group_map[0]]
    masked = masked.reshape(slot_count, 4, 2, part_rows, width)
    parity = column[:, None, None, None, None] * pick(masked, core, 2)[None]
    away = column[:, None, None, None, None] * pick(masked, 1 - core, 2)[None]
    parity = parity + swap(away, "core")
    for axis in ("yl", "ym"):
        place = lax.axis_index(axis)
        parity = parity.reshape(2, slot_count, -1, 2, part_rows, width) if axis == "yl" else parity
        parity = pick(parity, place, -3) + swap(pick(parity, 1 - place, -3), axis)
    parity_shards = parity[None, None]

    half = hot_rows // 2
    theirs = partial_grad(batch_ids[0, 0], out_grad[0, 0], (1 - core) * half, half)
    arrived = swap(theirs, "core")
    grad = partial_grad(batch_ids[0, 0], out_grad[0, 0], core * half, half) + arrived
    near = size(NEAR)
    grad = exchange(grad.reshape(near, half // near, width), NEAR).sum(axis=0)
    grad = to_all(grad, FAR).sum(axis=0)
    grad = to_all(grad, NEAR).reshape(half, width)
    other = swap(grad, "core")
    low, high = jnp.where(core == 0, grad, other), jnp.where(core == 0, other, grad)
    grad = jnp.concatenate([low, high], axis=0)
    new_weights, new_accum = adagrad(grad, hot_weights, accum)
    return (parity_shards, new_weights, new_accum)


def solution(mesh):
    mesh = Mesh(mesh.devices.reshape(SIZES), NAMES)
    in_specs = (
        P(CODE, DP, None, None, None),
        P(CODE, DP, None),
        P(CODE, DP),
        P(CODE),
        P(),
        P(CODE, DP, None),
        P(CODE, DP, None, None),
        P(),
        P(),
    )
    out_specs = (P(CODE, DP, None, None, None, None), P(), P())
    return jax.shard_map(shards, mesh=mesh, in_specs=in_specs, out_specs=out_specs, check_vma=False)
```

time: 421 us -> 129 us (0.31)
  waiting for transfers between devices: 367 us -> 46 us
  starting transfers between devices: 20.1 us -> 55.4 us
  between operations: 15.6 us -> 2.22 us
    psum x1 -> x0, waiting for transfers between devices: 316 us -> none  [shards(): grad = lax.psum(local_grad, ('code', 'dp'))]
    all_to_all x0 -> x3, starting transfers between devices: none -> 26.8 us  [exchange(): return lax.all_to_all(parts, axes, 0, 0, tiled=True)]
    ppermute x3 -> x5, waiting for transfers between devices: 50.6 us -> 25.1 us  [swap(): return lax.ppermute(value, axis, [(0, 1), (1, 0)])]
    all_to_all x0 -> x3, waiting for transfers between devices: none -> 21 us  [exchange(): return lax.all_to_all(parts, axes, 0, 0, tiled=True)]
    ppermute x3 -> x5, starting transfers between devices: 20 us -> 28.6 us  [swap(): return lax.ppermute(value, axis, [(0, 1), (1, 0)])]
    dot_general x1 -> x2, matrix products: 7.83 us -> 10.9 us  [partial_grad(): lax.dot_general(onehot, rows_grad, (((0,), (0,)), ((), ())), precision=la...]
  transfers between devices with their start and end apart: 4 -> 8, of which waited for: 3 -> 5; matrix products, arithmetic and copies ran while one was open for 3% -> 7% of each run, Pallas kernels for 0% -> 0%
where the time goes in v1:
time: 129 us; the launch traced here: 128 us
  starting transfers between devices  55.4 us (43%)
  waiting for transfers between devices  46 us (36%)
  matrix products  10.9 us (8%)
  other arithmetic  8.82 us (7%)
  local copies, waits for them, and re-layouts  4.64 us (4%)
  between operations  2.22 us (2%)
    ppermute x5, starting transfers between devices, swap(): return lax.ppermute(value, axis, [(0, 1), (1, 0)])  28.6 us
    all_to_all x3, starting transfers between devices, exchange(): return lax.all_to_all(parts, axes, 0, 0, tiled=True)  26.8 us
    ppermute x5, waiting for transfers between devices, swap(): return lax.ppermute(value, axis, [(0, 1), (1, 0)])  25.1 us
    all_to_all x3, waiting for transfers between devices, exchange(): return lax.all_to_all(parts, axes, 0, 0, tiled=True)  21 us
    dot_general x2, matrix products, partial_grad(): lax.dot_general(onehot, rows_grad, (((0,), (0,)), ((), ())), precision=la...  10.9 us
  transfers between devices with their start and end apart: 8, of which 5 were waited for; matrix products, arithmetic and copies ran while one was open for 7% of the time, Pallas kernels for 0%

profile of v1, /device:TPU:1, one launch (start us, length us, event | category | flops | bytes accessed | tf_op | source)
XLA Modules:
  0.0 128.0 jit_solution(3420826930713181066)
XLA Ops:
  0.7 0.8 broadcast_subtract_fusion.1
  1.4 5.4 %fusion.1 = f32[1024,128]{1,0:T(8,128)} fusion(s32[1024]{0:T(1024)S(1)} %bitcast.46, f32[1,1,1024,128]{3,2,1,0:T(8,128)} %param.15), kind=kOutput, calls=%fused_computation.4 | convolution fusion | flops 1611661312 | bytes 1052672 | tf_op jit(solution)/shard_map/dot_general | solution.py:42
  6.9 16.1 %collective-permute-start.3 = (f32[1024,128]{1,0:T(8,128)}, f32[1024,128]{1,0:T(8,128)}, u32[]{:S(2)}, u32[]{:S(2)}) collective-permute-start(f32[1024,128]{1,0:T(8,128)} %fusion.1), channel_id=1, source_target_pairs={{0,16},{16,0},{1,17},{17,1},{2,18},{18,2},{3,19},{19,3},{4,20},{20... | collective-permute-start | bytes 1572872 | tf_op jit(solution)/shard_map/ppermute | solution.py:27
  23.6 0.6 gather_fusion
  24.3 0.5 collective-permute-done.3
  24.8 5.4 %fusion.4 = f32[1024,128]{1,0:T(8,128)} fusion(f32[1024,128]{1,0:T(8,128)} %collective-permute-done.3, s32[1024]{0:T(1024)S(1)} %bitcast.45, f32[1,1,1024,128]{3,2,1,0:T(8,128)S(1)} %copy-done.6), kind=kOutput, calls=%fused_computation.7 | convolution fusion | flops 1611792384 | bytes 1576960 | tf_op jit(solution)/shard_map/dot_general | solution.py:42
  30.2 7.1 %all-to-all-start = ((f32[32,32,128]{2,1,0:T(8,128)}), f32[32,32,128]{2,1,0:T(8,128)}, u32[]{:S(2)}, u32[]{:S(2)}) async-start(f32[32,32,128]{2,1,0:T(8,128)} %bitcast.17), calls=%async_computation | async-start | bytes 1048576 | tf_op jit(solution)/shard_map/all_to_all | solution.py:19
  37.3 0.2 broadcast_multiply_fusion.1
  38.2 0.2 fusion.8
  38.3 0.9 dynamic-slice_bitcast_fusion.2
  39.2 1.2 broadcast_multiply_fusion
  40.4 2.5 %collective-permute-start = (f32[2,4,4,64,128]{4,3,2,1,0:T(8,128)}, f32[2,4,4,64,128]{4,3,2,1,0:T(8,128)S(1)}, u32[]{:S(2)}, u32[]{:S(2)}) collective-permute-start(f32[2,4,4,64,128]{4,3,2,1,0:T(8,128)} %broadcast_multiply_fusion), channel_id=1, source_target_pairs={{0,16},{16,0},{1,17},{17,1},{2,18},{18,2},{3,19},{19,3},{4,20},{20... | collective-permute-start | bytes 3145736 | tf_op jit(solution)/shard_map/ppermute | solution.py:27
  42.9 9.4 %all-to-all-done = f32[32,32,128]{2,1,0:T(8,128)} async-done(((f32[32,32,128]{2,1,0:T(8,128)}), f32[32,32,128]{2,1,0:T(8,128)}, u32[]{:S(2)}, u32[]{:S(2)}) %all-to-all-start) | async-done | bytes 524320 | tf_op jit(solution)/shard_map/all_to_all | solution.py:19
  52.3 1.1 reduce_sum.27
  53.4 0.7 broadcast_in_dim.7
  54.1 9.6 %all-to-all-start.1 = ((f32[16,32,128]{2,1,0:T(8,128)}), f32[16,32,128]{2,1,0:T(8,128)S(1)}, u32[]{:S(2)}, u32[]{:S(2)}) async-start(f32[16,32,128]{2,1,0:T(8,128)} %broadcast_in_dim.7), calls=%async_computation.1 | async-start | bytes 524288 | tf_op jit(solution)/shard_map/all_to_all | solution.py:19
  63.8 11.6 %all-to-all-done.1 = f32[16,32,128]{2,1,0:T(8,128)S(1)} async-done(((f32[16,32,128]{2,1,0:T(8,128)}), f32[16,32,128]{2,1,0:T(8,128)S(1)}, u32[]{:S(2)}, u32[]{:S(2)}) %all-to-all-start.1) | async-done | bytes 262176 | tf_op jit(solution)/shard_map/all_to_all | solution.py:19
  75.3 0.8 broadcast_in_dim.8
  76.2 10.1 %all-to-all-start.2 = ((f32[32,32,128]{2,1,0:T(8,128)}), f32[32,32,128]{2,1,0:T(8,128)S(1)}, u32[]{:S(2)}, u32[]{:S(2)}) async-start(f32[32,32,128]{2,1,0:T(8,128)} %broadcast_in_dim.8), calls=%async_computation.2 | async-start | bytes 1048576 | tf_op jit(solution)/shard_map/all_to_all | solution.py:19
  86.4 1.0 copy-done.3
  87.3 1.4 %multiply_add_fusion = f32[2,4,4,64,128]{4,3,2,1,0:T(8,128)S(1)} fusion(f32[2,4,4,64,128]{4,3,2,1,0:T(8,128)} %copy-done.3, f32[4,4,64,128]{3,2,1,0:T(8,128)S(1)} %copy-done.1, f32[2]{0:T(128)S(1)} %fusion.8), kind=kLoop, calls=%fused_computation.11 | loop fusion | flops 524288 | bytes 2621448 | tf_op jit(solution)/shard_map/add | solution.py:65
  88.8 2.7 %collective-permute-start.1 = (f32[2,4,2,64,128]{4,3,2,1,0:T(8,128)S(1)}, f32[2,4,2,64,128]{4,3,2,1,0:T(8,128)}, u32[]{:S(2)}, u32[]{:S(2)}) collective-permute-start(f32[2,4,2,64,128]{4,3,2,1,0:T(8,128)S(1)} %dynamic-slice_bitcast_fusion), channel_id=1, source_target_pairs={{0,32},{32,0},{1,33},{33,1},{2,34},{34,2},{3,35},{35,3},{4,36},{36... | collective-permute-start | bytes 1572872 | tf_op jit(solution)/shard_map/ppermute | solution.py:27
  91.5 11.6 %collective-permute-done.1 = f32[2,4,2,64,128]{4,3,2,1,0:T(8,128)} collective-permute-done((f32[2,4,2,64,128]{4,3,2,1,0:T(8,128)S(1)}, f32[2,4,2,64,128]{4,3,2,1,0:T(8,128)}, u32[]{:S(2)}, u32[]{:S(2)}) %collective-permute-start.1) | collective-permute-done | bytes 524320 | tf_op jit(solution)/shard_map/ppermute | solution.py:27
  103.1 1.1 bitcast_add_fusion
  104.2 3.9 %collective-permute-start.4 = (f32[1024,128]{1,0:T(8,128)S(1)}, f32[1024,128]{1,0:T(8,128)S(1)}, u32[]{:S(2)}, u32[]{:S(2)}) collective-permute-start(f32[1024,128]{1,0:T(8,128)S(1)} %bitcast.44), channel_id=1, source_target_pairs={{0,16},{16,0},{1,17},{17,1},{2,18},{18,2},{3,19},{19,3},{4,20},{20... | collective-permute-start | bytes 1572872 | tf_op jit(solution)/shard_map/ppermute | solution.py:27
  108.2 3.3 %collective-permute-start.2 = (f32[2,4,64,128]{3,2,1,0:T(8,128)S(1)}, f32[2,4,64,128]{3,2,1,0:T(8,128)S(1)}, u32[]{:S(2)}, u32[]{:S(2)}) collective-permute-start(f32[2,4,64,128]{3,2,1,0:T(8,128)S(1)} %dynamic-slice_bitcast_fusion.3), channel_id=1, source_target_pairs={{0,64},{64,0},{1,65},{65,1},{2,66},{66,2},{3,67},{67,3},{4,68},{68... | collective-permute-start | bytes 786440 | tf_op jit(solution)/shard_map/ppermute | solution.py:27
  111.6 13.0 %collective-permute-done.2 = f32[2,4,64,128]{3,2,1,0:T(8,128)S(1)} collective-permute-done((f32[2,4,64,128]{3,2,1,0:T(8,128)S(1)}, f32[2,4,64,128]{3,2,1,0:T(8,128)S(1)}, u32[]{:S(2)}, u32[]{:S(2)}) %collective-permute-start.2) | collective-permute-done | bytes 262176 | tf_op jit(solution)/shard_map/ppermute | solution.py:27
  124.5 0.7 fusion.7
  125.4 0.3 multiply_reduce_fusion
  125.7 0.3 copy-done.4
  126.0 0.6 sqrt_add_fusion
  126.7 1.3 %divide_subtract_fusion = f32[2048,128]{1,0:T(8,128)} fusion(f32[2048,128]{1,0:T(8,128)S(1)} %copy-done.2, f32[1024,128]{1,0:T(8,128)S(1)} %get-tuple-element.6, f32[1024,128]{1,0:T(8,128)S(1)} %get-tuple-element.5, f32[2048]{0:T(1024)S(1)} %get-tuple-element.3), kind=kLoop, calls=%fused_computation.9 | loop fusion | flops 1048576 | bytes 3153920 | tf_op jit(solution)/shard_map/sub | solution.py:36
  (24 shorter events, 0.2 us)
Async XLA Ops:
  0.6 23.0 %copy-start = (f32[1,1,4,512,128]{4,3,2,1,0:T(8,128)S(1)}, f32[1,1,4,512,128]{4,3,2,1,0:T(8,128)}, u32[]{:S(2)}) copy-start(f32[1,1,4,512,128]{4,3,2,1,0:T(8,128)} %param.9) | copy-start | bytes 3145732
  0.6 22.9 %copy-start.7 = (s32[1,1,4]{2,1,0:T(1,128)S(1)}, s32[1,1,4]{2,1,0:T(1,128)}, u32[]{:S(2)}) copy-start(s32[1,1,4]{2,1,0:T(1,128)} %param.10) | copy-start | bytes 52
  6.9 17.9 %collective-permute-start.3 = (f32[1024,128]{1,0:T(8,128)}, f32[1024,128]{1,0:T(8,128)}, u32[]{:S(2)}, u32[]{:S(2)}) collective-permute-start(f32[1024,128]{1,0:T(8,128)} %fusion.1), channel_id=1, source_target_pairs={{0,16},{16,0},{1,17},{17,1},{2,18},{18,2},{3,19},{19,3},{4,20},{20... | collective-permute-start | bytes 1572872 | tf_op jit(solution)/shard_map/ppermute | solution.py:27
  23.6 1.2 copy-start.6
  30.2 22.1 %all-to-all-start = ((f32[32,32,128]{2,1,0:T(8,128)}), f32[32,32,128]{2,1,0:T(8,128)}, u32[]{:S(2)}, u32[]{:S(2)}) async-start(f32[32,32,128]{2,1,0:T(8,128)} %bitcast.17), calls=%async_computation | async-start | bytes 1048576 | tf_op jit(solution)/shard_map/all_to_all | solution.py:19
  37.3 0.9 copy-start.5
  40.4 46.0 %collective-permute-start = (f32[2,4,4,64,128]{4,3,2,1,0:T(8,128)}, f32[2,4,4,64,128]{4,3,2,1,0:T(8,128)S(1)}, u32[]{:S(2)}, u32[]{:S(2)}) collective-permute-start(f32[2,4,4,64,128]{4,3,2,1,0:T(8,128)} %broadcast_multiply_fusion), channel_id=1, source_target_pairs={{0,16},{16,0},{1,17},{17,1},{2,18},{18,2},{3,19},{19,3},{4,20},{20... | collective-permute-start | bytes 3145736 | tf_op jit(solution)/shard_map/ppermute | solution.py:27
  54.1 21.2 %all-to-all-start.1 = ((f32[16,32,128]{2,1,0:T(8,128)}), f32[16,32,128]{2,1,0:T(8,128)S(1)}, u32[]{:S(2)}, u32[]{:S(2)}) async-start(f32[16,32,128]{2,1,0:T(8,128)} %broadcast_in_dim.7), calls=%async_computation.1 | async-start | bytes 524288 | tf_op jit(solution)/shard_map/all_to_all | solution.py:19
  63.7 23.6 %copy-start.1 = (f32[4,4,64,128]{3,2,1,0:T(8,128)S(1)}, f32[4,4,64,128]{3,2,1,0:T(8,128)}, u32[]{:S(2)}) copy-start(f32[4,4,64,128]{3,2,1,0:T(8,128)} %get-tuple-element.7) | copy-start | bytes 1572868
  76.2 28.0 %all-to-all-start.2 = ((f32[32,32,128]{2,1,0:T(8,128)}), f32[32,32,128]{2,1,0:T(8,128)S(1)}, u32[]{:S(2)}, u32[]{:S(2)}) async-start(f32[32,32,128]{2,1,0:T(8,128)} %broadcast_in_dim.8), calls=%async_computation.2 | async-start | bytes 1048576 | tf_op jit(solution)/shard_map/all_to_all | solution.py:19
  86.3 1.0 copy-start.3
  88.8 14.3 %collective-permute-start.1 = (f32[2,4,2,64,128]{4,3,2,1,0:T(8,128)S(1)}, f32[2,4,2,64,128]{4,3,2,1,0:T(8,128)}, u32[]{:S(2)}, u32[]{:S(2)}) collective-permute-start(f32[2,4,2,64,128]{4,3,2,1,0:T(8,128)S(1)} %dynamic-slice_bitcast_fusion), channel_id=1, source_target_pairs={{0,32},{32,0},{1,33},{33,1},{2,34},{34,2},{3,35},{35,3},{4,36},{36... | collective-permute-start | bytes 1572872 | tf_op jit(solution)/shard_map/ppermute | solution.py:27
  104.2 21.0 %collective-permute-start.4 = (f32[1024,128]{1,0:T(8,128)S(1)}, f32[1024,128]{1,0:T(8,128)S(1)}, u32[]{:S(2)}, u32[]{:S(2)}) collective-permute-start(f32[1024,128]{1,0:T(8,128)S(1)} %bitcast.44), channel_id=1, source_target_pairs={{0,16},{16,0},{1,17},{17,1},{2,18},{18,2},{3,19},{19,3},{4,20},{20... | collective-permute-start | bytes 1572872 | tf_op jit(solution)/shard_map/ppermute | solution.py:27
  108.2 16.3 %collective-permute-start.2 = (f32[2,4,64,128]{3,2,1,0:T(8,128)S(1)}, f32[2,4,64,128]{3,2,1,0:T(8,128)S(1)}, u32[]{:S(2)}, u32[]{:S(2)}) collective-permute-start(f32[2,4,64,128]{3,2,1,0:T(8,128)S(1)} %dynamic-slice_bitcast_fusion.3), channel_id=1, source_target_pairs={{0,64},{64,0},{1,65},{65,1},{2,66},{66,2},{3,67},{67,3},{4,68},{68... | collective-permute-start | bytes 786440 | tf_op jit(solution)/shard_map/ppermute | solution.py:27
  125.3 0.7 copy-start.4
  125.4 1.3 %copy-start.2 = (f32[2048,128]{1,0:T(8,128)S(1)}, f32[2048,128]{1,0:T(8,128)}, u32[]{:S(2)}) copy-start(f32[2048,128]{1,0:T(8,128)} %param.16) | copy-start | bytes 3145732

commit v2 on v1

v2 whole, which is shorter than its diff:
```python
import jax
import jax.numpy as jnp
from jax import lax
from jax.experimental import pallas as pl
from jax.experimental.pallas import tpu as pltpu
from jax.sharding import Mesh, PartitionSpec as P

NAMES = ("xh", "xm", "yh", "ym", "yl", "core", "xl", "z")
SIZES = (2, 2, 2, 2, 2, 2, 2, 8)
CODE = ("xh", "xm", "yh", "ym", "yl", "core")
DP = ("xl", "z")
NEAR = ("xm", "xl", "z")
TILE = 256
FAR = ("xh", "yh", "ym", "yl")


def size(axes):
    return lax.axis_size(axes)


def exchange(parts, axes):
    return lax.all_to_all(parts, axes, 0, 0, tiled=True)


def sum_copies_kernel(parts_ref, ready_ref, copies_ref):
    total = parts_ref[0]
    for part in range(1, parts_ref.shape[0]):
        total = total + parts_ref[part]
    copies_ref[...] = jnp.broadcast_to(total[None], copies_ref.shape)


def sum_copies(parts, copies, ready):
    shape = (copies,) + parts.shape[1:]
    return pl.pallas_call(
        sum_copies_kernel,
        out_shape=jax.ShapeDtypeStruct(shape, jnp.float32),
        in_specs=[pl.BlockSpec(memory_space=pltpu.VMEM), pl.BlockSpec(memory_space=pl.ANY)],
        out_specs=pl.BlockSpec(memory_space=pltpu.VMEM),
        cost_estimate=pl.CostEstimate(flops=parts.size, bytes_accessed=4 * parts.size, transcendentals=0),
        compiler_params=pltpu.CompilerParams(vmem_limit_bytes=24 << 20),
        name="sum_copies",
    )(parts, ready)


def swap(value, axis):
    return lax.ppermute(value, axis, [(0, 1), (1, 0)])


def pick(value, place, axis):
    return lax.dynamic_index_in_dim(value, place, axis, keepdims=False)


def sum_kernel(first_ref, ids_ref, rows_ref, out_ref):
    width = rows_ref.shape[1]
    value = rows_ref[...]
    high = value.astype(jnp.bfloat16)
    rest = value - high.astype(jnp.float32)
    middle = rest.astype(jnp.bfloat16)
    low = (rest - middle.astype(jnp.float32)).astype(jnp.bfloat16)
    three = jnp.concatenate([high, middle, low], axis=1)
    ids = ids_ref[...] - first_ref[0]
    for tile in range(out_ref.shape[0] // TILE):
        row = lax.broadcasted_iota(jnp.int32, (TILE, ids.shape[1]), 0) + tile * TILE
        hit = jnp.where(row == ids, 1.0, 0.0).astype(jnp.bfloat16)
        part = jnp.dot(hit, three, preferred_element_type=jnp.float32)
        total = part[:, :width] + part[:, width : 2 * width] + part[:, 2 * width :]
        out_ref[tile * TILE : (tile + 1) * TILE, :] = total


def partial_grad(ids, rows_grad, first, rows):
    lookups, width = rows_grad.shape
    return pl.pallas_call(
        sum_kernel,
        out_shape=jax.ShapeDtypeStruct((rows, width), jnp.float32),
        in_specs=[
            pl.BlockSpec(memory_space=pltpu.SMEM),
            pl.BlockSpec(memory_space=pltpu.VMEM),
            pl.BlockSpec(memory_space=pltpu.VMEM),
        ],
        out_specs=pl.BlockSpec(memory_space=pltpu.VMEM),
        cost_estimate=pl.CostEstimate(flops=6 * rows * lookups * width, bytes_accessed=4 * (lookups + rows) * width, transcendentals=0),
        compiler_params=pltpu.CompilerParams(vmem_limit_bytes=24 << 20),
        name="hot_rows_sum",
    )(first.reshape(1), ids.reshape(1, lookups), rows_grad)


def coded_kernel(ids_ref, counts_ref, column_ref, core_ref, coef_ref, cold_ref, ready_ref, kept_ref, sent_ref):
    slot, core, column = pl.program_id(0), core_ref[0], column_ref[0]
    live = jnp.where(slot < counts_ref[0], 1.0, 0.0)
    kept, sent = cold_ref[0, :, core] * live, cold_ref[0, :, 1 - core] * live
    for parity in range(kept_ref.shape[0]):
        kept_ref[parity, 0] = coef_ref[parity, column] * kept
        sent_ref[parity, 0] = coef_ref[parity, column] * sent


def coded(cold_table, block_ids, counts, group_map, coef, core, ready):
    parities, slots = coef.shape[0], block_ids.shape[0]
    rest = cold_table.shape[1:]
    shape = (parities, slots, rest[0]) + rest[2:]
    out = pl.BlockSpec((parities, 1) + shape[2:], lambda s, *refs: (0, s, 0, 0, 0))
    return pl.pallas_call(
        coded_kernel,
        grid_spec=pltpu.PrefetchScalarGridSpec(
            num_scalar_prefetch=4,
            grid=(slots,),
            in_specs=[
                pl.BlockSpec(memory_space=pltpu.SMEM),
                pl.BlockSpec((1,) + rest, lambda s, ids, *refs: (ids[s], 0, 0, 0, 0)),
                pl.BlockSpec(memory_space=pl.ANY),
            ],
            out_specs=[out, out],
        ),
        out_shape=[jax.ShapeDtypeStruct(shape, jnp.float32)] * 2,
        cost_estimate=pl.CostEstimate(flops=cold_table.size * 3, bytes_accessed=12 * cold_table.size, transcendentals=0),
        compiler_params=pltpu.CompilerParams(vmem_limit_bytes=24 << 20),
        name="coded_blocks",
    )(block_ids, counts, group_map, core.reshape(1), coef, cold_table, ready)


def adagrad_kernel(place_ref, grad_ref, weights_ref, accum_ref, *refs):
    new_weights_ref, new_accum_ref = refs[-2:]
    for block in range(8):
        rows = slice(block * 128, (block + 1) * 128)
        grad = grad_ref[rows, :]
        mean = jnp.mean(grad * grad, axis=1, keepdims=True)
        accum = jnp.transpose(jnp.broadcast_to(accum_ref[block : block + 1, :], (128, 128)))
        new_accum = accum + mean
        new_weights_ref[rows, :] = weights_ref[rows, :] - 0.5 * grad / (jnp.sqrt(new_accum) + 1e-06)
        new_accum_ref[block : block + 1, :] = jnp.transpose(new_accum)[:1, :]


def adagrad_half(place, grad, weights, accum, before=None):
    half, width = grad.shape
    at = lambda i, place: (place[0], 0)
    given = () if before is None else tuple(before)
    return pl.pallas_call(
        adagrad_kernel,
        grid_spec=pltpu.PrefetchScalarGridSpec(
            num_scalar_prefetch=1,
            grid=(1,),
            in_specs=[
                pl.BlockSpec((half, width), lambda i, place: (0, 0)),
                pl.BlockSpec((half, width), at),
                pl.BlockSpec((half // width, width), at),
            ]
            + [pl.BlockSpec(memory_space=pl.ANY)] * len(given),
            out_specs=[pl.BlockSpec((half, width), at), pl.BlockSpec((half // width, width), at)],
        ),
        out_shape=[jax.ShapeDtypeStruct(weights.shape, jnp.float32), jax.ShapeDtypeStruct(accum.shape, jnp.float32)],
        input_output_aliases={4: 0, 5: 1} if given else {},
        cost_estimate=pl.CostEstimate(flops=8 * half * width, bytes_accessed=12 * half * width, transcendentals=half * width),
        compiler_params=pltpu.CompilerParams(vmem_limit_bytes=24 << 20),
        name="hot_rows_adagrad",
    )(place.reshape(1), grad, weights, accum, *given)


def shards(cold_table, block_ids, counts, group_map, coef, batch_ids, out_grad, hot_weights, accum):
    slot_count = block_ids.shape[2]
    block_rows = cold_table.shape[3]
    width = cold_table.shape[4]
    hot_rows = hot_weights.shape[0]
    part_rows = block_rows // 8
    core = lax.axis_index("core")

    half = hot_rows // 2
    theirs = partial_grad(batch_ids[0, 0], out_grad[0, 0], (1 - core) * half, half)
    arrived = swap(theirs, "core")

    table = cold_table[0, 0].reshape(-1, 4, 2, part_rows, width)
    parity, away = coded(table, block_ids[0, 0], counts[0], group_map, coef, core, theirs)
    parity = parity + swap(away, "core")
    parity = parity.reshape(2, slot_count, 2, 2, part_rows, width)
    near_y, far_y = lax.axis_index("yl"), lax.axis_index("ym")
    send_near = pick(parity, 1 - near_y, 3)
    parity = pick(parity, near_y, 3) + swap(send_near, "yl")
    send_far = pick(parity, 1 - far_y, 2)
    parity_shards = (pick(parity, far_y, 2) + swap(send_far, "ym"))[None, None]

    grad = partial_grad(batch_ids[0, 0], out_grad[0, 0], core * half, half) + arrived
    near = size(NEAR)
    parts = exchange(grad.reshape(near, half // near, width), NEAR)
    parts = exchange(sum_copies(parts, size(FAR), send_near), FAR)
    grad = exchange(sum_copies(parts, near, send_far), NEAR).reshape(half, width)
    grad, parity_shards = lax.optimization_barrier((grad, parity_shards))
    other = swap(grad, "core")
    sums = accum.reshape(hot_rows // width, width)
    done = adagrad_half(core, grad, hot_weights, sums)
    new_weights, new_accum = adagrad_half(1 - core, other, hot_weights, sums, done)
    new_accum = new_accum.reshape(hot_rows)
    return (parity_shards, new_weights, new_accum)


def solution(mesh):
    mesh = Mesh(mesh.devices.reshape(SIZES), NAMES)
    in_specs = (
        P(CODE, DP, None, None, None),
        P(CODE, DP, None),
        P(CODE, DP),
        P(CODE),
        P(),
        P(CODE, DP, None),
        P(CODE, DP, None, None),
        P(),
        P(),
    )
    out_specs = (P(CODE, DP, None, None, None, None), P(), P())
    return jax.shard_map(shards, mesh=mesh, in_specs=in_specs, out_specs=out_specs, check_vma=False)
```

time: 129 us -> 107 us (0.83)
  matrix products: 10.9 us -> 0 us
  waiting for transfers between devices: 46 us -> 35.7 us
  Pallas kernels: 0 us -> 8.3 us
  other arithmetic: 8.82 us -> 4.06 us
  local copies, waits for them, and re-layouts: 4.64 us -> 2.47 us
  starting transfers between devices: 55.4 us -> 53.8 us
    ppermute x5, waiting for transfers between devices: 25.1 us -> 13.8 us  [swap(): return lax.ppermute(value, axis, [(0, 1), (1, 0)])]
    dot_general x2 -> x0, matrix products: 10.9 us -> none  [partial_grad(): lax.dot_general(onehot, rows_grad, (((0,), (0,)), ((), ())), precision=la...]
    pallas_call x0 -> x7, Pallas kernels: none -> 8.3 us  [the longest x2 2.61 us: adagrad_half(): pl.pallas_call(adagrad_kernel, grid_spec=pltpu.PrefetchScalarGridSpec(num...]
    sub x2 -> x0, other arithmetic: 2.09 us -> none  [the longest x1 1.31 us: adagrad(): updated = weights - 0.5 * grad / (jnp.sqrt(updated_accum)[:, None] + 1e-06)]
    broadcast_in_dim x2 -> x0, local copies, waits for them, and re-layouts: 1.57 us -> none  [to_all(): jnp.broadcast_to(block[None], (size(axes),) + block.shape)]
    reduce_sum x3 -> x0, other arithmetic: 1.45 us -> none  [the longest x1 1.09 us: shards(): grad = exchange(grad.reshape(near, half // near, width), NEAR).sum(axis=0)]
    mul x2 -> x0, other arithmetic: 1.34 us -> none  [the longest x1 1.16 us: shards(): away = column[:, None, None, None, None] * pick(masked, 1 - core, 2)[None]]
  transfers between devices with their start and end apart: 8 -> 8, of which waited for: 5 -> 5; matrix products, arithmetic and copies ran while one was open for 7% -> 4% of each run, Pallas kernels for 0% -> 3%
where the time goes in v2:
time: 107 us; the launch traced here: 106 us
  starting transfers between devices  53.8 us (50%)
  waiting for transfers between devices  35.7 us (33%)
  Pallas kernels  8.3 us (8%)
  other arithmetic  4.06 us (4%)
  local copies, waits for them, and re-layouts  2.47 us (2%)
  between operations  2.13 us (2%)
    ppermute x5, starting transfers between devices, swap(): return lax.ppermute(value, axis, [(0, 1), (1, 0)])  27.4 us
    all_to_all x3, starting transfers between devices, exchange(): return lax.all_to_all(parts, axes, 0, 0, tiled=True)  26.4 us
    all_to_all x3, waiting for transfers between devices, exchange(): return lax.all_to_all(parts, axes, 0, 0, tiled=True)  21.8 us
    ppermute x5, waiting for transfers between devices, swap(): return lax.ppermute(value, axis, [(0, 1), (1, 0)])  13.8 us
    pallas_call x2, Pallas kernels, adagrad_half(): pl.pallas_call(adagrad_kernel, grid_spec=pltpu.PrefetchScalarGridSpec(num...  2.61 us
    pallas_call x2, Pallas kernels, partial_grad(): pl.pallas_call(sum_kernel, out_shape=jax.ShapeDtypeStruct((rows, width),...  2.54 us
    unnamed x16, local copies, waits for them, and re-layouts  2.39 us
  transfers between devices with their start and end apart: 8, of which 5 were waited for; matrix products, arithmetic and copies ran while one was open for 4% of the time, Pallas kernels for 3%

profile of v2, /device:TPU:1, one launch (start us, length us, event | category | flops | bytes accessed | tf_op | source)
XLA Modules:
  0.0 106.5 jit_solution(8700189561073648294)
XLA Ops:
  1.9 0.7 copy-done.7
  2.6 1.0 copy-done.5
  3.7 1.3 %hot_rows_sum.3.ready_ref = f32[1024,128]{1,0:T(8,128)S(1)} custom-call(s32[1]{0:T(128)} %bitcast.3.first_ref, s32[1,1024]{1,0:T(1,128)S(1)} %bitcast.39, f32[1024,128]{1,0:T(8,128)S(1)} %bitcast.37), custom_call_target="tpu_custom_call" | custom-call | flops 805306368 | bytes 1048576 | tf_op jit(solution)/shard_map/hot_rows_sum/pallas_call | solution.py:72
  4.9 0.0 copy-start.3
  4.9 0.0 copy-start.4
  5.0 0.6 copy-done.3
  5.6 1.5 %coded_blocks.1 = (f32[2,4,4,64,128]{4,3,2,1,0:T(8,128)S(1)}, f32[2,4,4,64,128]{4,3,2,1,0:T(8,128)S(1)}) custom-call(s32[4]{0:T(128)S(1)} %bitcast.36, s32[1]{0:T(128)} %bitcast.30.counts_ref, s32[1]{0:T(128)S(6)} %copy.21.column_ref, s32[1]{0:T(128)} %bitcast.7.core_ref.place_ref, f32[2,8]{1,0:T(2,128)S(1)} %copy-done.3, ...), custom_call_target="tpu_custom_call" | custom-call | flops 786432 | bytes 3145728 | tf_op jit(solution)/shard_map/coded_blocks/pallas_call | solution.py:101
  7.1 16.1 %collective-permute-start.1 = (f32[2,4,4,64,128]{4,3,2,1,0:T(8,128)S(1)}, f32[2,4,4,64,128]{4,3,2,1,0:T(8,128)}, u32[]{:S(2)}, u32[]{:S(2)}) collective-permute-start(f32[2,4,4,64,128]{4,3,2,1,0:T(8,128)S(1)} %get-tuple-element.12), channel_id=1, source_target_pairs={{0,16},{16,0},{1,17},{17,1},{2,18},{18,2},{3,19},{19,3},{4,20},{20... | collective-permute-start | bytes 3145736 | tf_op jit(solution)/shard_map/ppermute | solution.py:46
  23.2 1.9 %collective-permute-start = (f32[1024,128]{1,0:T(8,128)S(1)}, f32[1024,128]{1,0:T(8,128)}, u32[]{:S(2)}, u32[]{:S(2)}) collective-permute-start(f32[1024,128]{1,0:T(8,128)S(1)} %hot_rows_sum.3.ready_ref), channel_id=1, source_target_pairs={{0,16},{16,0},{1,17},{17,1},{2,18},{18,2},{3,19},{19,3},{4,20},{20... | collective-permute-start | bytes 1572872 | tf_op jit(solution)/shard_map/ppermute | solution.py:46
  25.2 1.3 %hot_rows_sum.2 = f32[1024,128]{1,0:T(8,128)S(1)} custom-call(s32[1]{0:T(128)} %bitcast.first_ref, s32[1,1024]{1,0:T(1,128)S(1)} %bitcast.40, f32[1024,128]{1,0:T(8,128)S(1)} %bitcast.38), custom_call_target="tpu_custom_call" | custom-call | flops 805306368 | bytes 1048576 | tf_op jit(solution)/shard_map/hot_rows_sum/pallas_call | solution.py:72
  26.4 0.7 collective-permute-done
  27.2 1.9 %add.28 = f32[1024,128]{1,0:T(8,128)} add(f32[1024,128]{1,0:T(8,128)S(1)} %hot_rows_sum.2, f32[1024,128]{1,0:T(8,128)} %collective-permute-done) | non-fusion elementwise | flops 131072 | bytes 1572864 | tf_op jit(solution)/shard_map/add | solution.py:179
  29.0 6.9 %all-to-all-start = ((f32[32,32,128]{2,1,0:T(8,128)}), f32[32,32,128]{2,1,0:T(8,128)S(1)}, u32[]{:S(2)}, u32[]{:S(2)}) async-start(f32[32,32,128]{2,1,0:T(8,128)} %bitcast.4), calls=%async_computation | async-start | bytes 1048576 | tf_op jit(solution)/shard_map/all_to_all | solution.py:22
  36.0 0.0 collective-permute-done.1
  36.0 1.4 %add.29 = f32[2,4,4,64,128]{4,3,2,1,0:T(8,128)S(1)} add(f32[2,4,4,64,128]{4,3,2,1,0:T(8,128)S(1)} %get-tuple-element.11, f32[2,4,4,64,128]{4,3,2,1,0:T(8,128)} %collective-permute-done.1) | non-fusion elementwise | flops 262144 | bytes 3145728 | tf_op jit(solution)/shard_map/add | solution.py:171
  37.4 0.1 dynamic-slice_bitcast_fusion.ready_ref
  37.4 3.3 %collective-permute-start.2 = (f32[2,4,2,64,128]{4,3,2,1,0:T(8,128)S(1)}, f32[2,4,2,64,128]{4,3,2,1,0:T(8,128)S(1)}, u32[]{:S(2)}, u32[]{:S(2)}) collective-permute-start(f32[2,4,2,64,128]{4,3,2,1,0:T(8,128)S(1)} %dynamic-slice_bitcast_fusion.ready_ref), channel_id=1, source_target_pairs={{0,32},{32,0},{1,33},{33,1},{2,34},{34,2},{3,35},{35,3},{4,36},{36... | collective-permute-start | bytes 1572872 | tf_op jit(solution)/shard_map/ppermute | solution.py:46
  40.7 10.5 %all-to-all-done.parts_ref = f32[32,32,128]{2,1,0:T(8,128)S(1)} async-done(((f32[32,32,128]{2,1,0:T(8,128)}), f32[32,32,128]{2,1,0:T(8,128)S(1)}, u32[]{:S(2)}, u32[]{:S(2)}) %all-to-all-start) | async-done | bytes 524320 | tf_op jit(solution)/shard_map/all_to_all | solution.py:22
  51.3 0.8 sum_copies.2
  52.1 9.6 %all-to-all-start.1 = ((f32[16,32,128]{2,1,0:T(8,128)}), f32[16,32,128]{2,1,0:T(8,128)S(1)}, u32[]{:S(2)}, u32[]{:S(2)}) async-start(f32[16,32,128]{2,1,0:T(8,128)} %sum_copies.2), calls=%async_computation.1 | async-start | bytes 524288 | tf_op jit(solution)/shard_map/all_to_all | solution.py:22
  61.7 0.1 bitcast_add_fusion
  61.8 11.3 %all-to-all-done.1.parts_ref = f32[16,32,128]{2,1,0:T(8,128)S(1)} async-done(((f32[16,32,128]{2,1,0:T(8,128)}), f32[16,32,128]{2,1,0:T(8,128)S(1)}, u32[]{:S(2)}, u32[]{:S(2)}) %all-to-all-start.1) | async-done | bytes 262176 | tf_op jit(solution)/shard_map/all_to_all | solution.py:22
  73.1 0.9 sum_copies.3
  74.0 9.9 %all-to-all-start.2 = ((f32[32,32,128]{2,1,0:T(8,128)}), f32[32,32,128]{2,1,0:T(8,128)S(1)}, u32[]{:S(2)}, u32[]{:S(2)}) async-start(f32[32,32,128]{2,1,0:T(8,128)} %sum_copies.3), calls=%async_computation.2 | async-start | bytes 1048576 | tf_op jit(solution)/shard_map/all_to_all | solution.py:22
  83.9 3.2 %collective-permute-start.3 = (f32[2,4,64,128]{3,2,1,0:T(8,128)S(1)}, f32[2,4,64,128]{3,2,1,0:T(8,128)S(1)}, u32[]{:S(2)}, u32[]{:S(2)}) collective-permute-start(f32[2,4,64,128]{3,2,1,0:T(8,128)S(1)} %dynamic-slice_bitcast_fusion.1.ready_ref), channel_id=1, source_target_pairs={{0,64},{64,0},{1,65},{65,1},{2,66},{66,2},{3,67},{67,3},{4,68},{68... | collective-permute-start | bytes 786440 | tf_op jit(solution)/shard_map/ppermute | solution.py:46
  87.1 12.9 %collective-permute-done.3 = f32[2,4,64,128]{3,2,1,0:T(8,128)S(1)} collective-permute-done((f32[2,4,64,128]{3,2,1,0:T(8,128)S(1)}, f32[2,4,64,128]{3,2,1,0:T(8,128)S(1)}, u32[]{:S(2)}, u32[]{:S(2)}) %collective-permute-start.3) | collective-permute-done | bytes 262176 | tf_op jit(solution)/shard_map/ppermute | solution.py:46
  100.0 0.7 fusion
  100.7 0.0 all-to-all-done.2
  100.7 2.9 %collective-permute-start.4 = (f32[1024,128]{1,0:T(8,128)S(1)}, f32[1024,128]{1,0:T(8,128)S(1)}, u32[]{:S(2)}, u32[]{:S(2)}) collective-permute-start(f32[1024,128]{1,0:T(8,128)S(1)} %bitcast.31), channel_id=1, source_target_pairs={{0,16},{16,0},{1,17},{17,1},{2,18},{18,2},{3,19},{19,3},{4,20},{20... | collective-permute-start | bytes 1572872 | tf_op jit(solution)/shard_map/ppermute | solution.py:46
  103.7 1.3 %hot_rows_adagrad.2 = (f32[2048,128]{1,0:T(8,128)}, f32[16,128]{1,0:T(8,128)}) custom-call(s32[1]{0:T(128)} %bitcast.7.core_ref.place_ref, f32[1024,128]{1,0:T(8,128)S(1)} %bitcast.32, f32[2048,128]{1,0:T(8,128)S(1)} %copy-done, f32[16,128]{1,0:T(8,128)S(1)} %bitcast.34), custom_call_target="tpu_custom_call" | custom-call | flops 1048576 | bytes 1572864 | tf_op jit(solution)/shard_map/hot_rows_adagrad/pallas_call | solution.py:136
  105.0 0.2 collective-permute-done.4.grad_ref
  105.1 1.3 %hot_rows_adagrad.3 = (f32[2048,128]{1,0:T(8,128)}, f32[16,128]{1,0:T(8,128)}) custom-call(s32[1]{0:T(128)} %bitcast.16.place_ref, f32[1024,128]{1,0:T(8,128)S(1)} %collective-permute-done.4.grad_ref, f32[2048,128]{1,0:T(8,128)S(1)} %copy-done, f32[16,128]{1,0:T(8,128)S(1)} %bitcast.35, ...), custom_call_target="tpu_custom_call", output_to_operand_aliasing={{0}: (4, {}), {1}: (5, {})} | custom-call | flops 1048576 | bytes 1572864 | tf_op jit(solution)/shard_map/hot_rows_adagrad/pallas_call | solution.py:136
  (13 shorter events, 0.1 us)
Async XLA Ops:
  1.9 0.7 copy-start.7
  2.6 1.0 copy-start.5
  3.7 1.3 %copy-start.1 = (f32[1,1,4,512,128]{4,3,2,1,0:T(8,128)S(1)}, f32[1,1,4,512,128]{4,3,2,1,0:T(8,128)}, u32[]{:S(2)}) copy-start(f32[1,1,4,512,128]{4,3,2,1,0:T(8,128)} %param.9) | copy-start | bytes 3145732
  4.9 0.7 copy-start.3
  4.9 0.7 copy-start.4
  5.6 19.5 %copy-start.6 = (f32[1,1,1024,128]{3,2,1,0:T(8,128)S(1)}, f32[1,1,1024,128]{3,2,1,0:T(8,128)}, u32[]{:S(2)}) copy-start(f32[1,1,1024,128]{3,2,1,0:T(8,128)} %param.15) | copy-start | bytes 1572868
  7.1 28.8 %collective-permute-start.1 = (f32[2,4,4,64,128]{4,3,2,1,0:T(8,128)S(1)}, f32[2,4,4,64,128]{4,3,2,1,0:T(8,128)}, u32[]{:S(2)}, u32[]{:S(2)}) collective-permute-start(f32[2,4,4,64,128]{4,3,2,1,0:T(8,128)S(1)} %get-tuple-element.12), channel_id=1, source_target_pairs={{0,16},{16,0},{1,17},{17,1},{2,18},{18,2},{3,19},{19,3},{4,20},{20... | collective-permute-start | bytes 3145736 | tf_op jit(solution)/shard_map/ppermute | solution.py:46
  23.2 3.9 %collective-permute-start = (f32[1024,128]{1,0:T(8,128)S(1)}, f32[1024,128]{1,0:T(8,128)}, u32[]{:S(2)}, u32[]{:S(2)}) collective-permute-start(f32[1024,128]{1,0:T(8,128)S(1)} %hot_rows_sum.3.ready_ref), channel_id=1, source_target_pairs={{0,16},{16,0},{1,17},{17,1},{2,18},{18,2},{3,19},{19,3},{4,20},{20... | collective-permute-start | bytes 1572872 | tf_op jit(solution)/shard_map/ppermute | solution.py:46
  29.0 22.2 %all-to-all-start = ((f32[32,32,128]{2,1,0:T(8,128)}), f32[32,32,128]{2,1,0:T(8,128)S(1)}, u32[]{:S(2)}, u32[]{:S(2)}) async-start(f32[32,32,128]{2,1,0:T(8,128)} %bitcast.4), calls=%async_computation | async-start | bytes 1048576 | tf_op jit(solution)/shard_map/all_to_all | solution.py:22
  37.4 24.3 %collective-permute-start.2 = (f32[2,4,2,64,128]{4,3,2,1,0:T(8,128)S(1)}, f32[2,4,2,64,128]{4,3,2,1,0:T(8,128)S(1)}, u32[]{:S(2)}, u32[]{:S(2)}) collective-permute-start(f32[2,4,2,64,128]{4,3,2,1,0:T(8,128)S(1)} %dynamic-slice_bitcast_fusion.ready_ref), channel_id=1, source_target_pairs={{0,32},{32,0},{1,33},{33,1},{2,34},{34,2},{3,35},{35,3},{4,36},{36... | collective-permute-start | bytes 1572872 | tf_op jit(solution)/shard_map/ppermute | solution.py:46
  52.1 21.0 %all-to-all-start.1 = ((f32[16,32,128]{2,1,0:T(8,128)}), f32[16,32,128]{2,1,0:T(8,128)S(1)}, u32[]{:S(2)}, u32[]{:S(2)}) async-start(f32[16,32,128]{2,1,0:T(8,128)} %sum_copies.2), calls=%async_computation.1 | async-start | bytes 524288 | tf_op jit(solution)/shard_map/all_to_all | solution.py:22
  74.0 29.7 %copy-start = (f32[2048,128]{1,0:T(8,128)S(1)}, f32[2048,128]{1,0:T(8,128)}, u32[]{:S(2)}) copy-start(f32[2048,128]{1,0:T(8,128)} %weights_ref.3) | copy-start | bytes 3145732
  74.0 26.8 %all-to-all-start.2 = ((f32[32,32,128]{2,1,0:T(8,128)}), f32[32,32,128]{2,1,0:T(8,128)S(1)}, u32[]{:S(2)}, u32[]{:S(2)}) async-start(f32[32,32,128]{2,1,0:T(8,128)} %sum_copies.3), calls=%async_computation.2 | async-start | bytes 1048576 | tf_op jit(solution)/shard_map/all_to_all | solution.py:22
  83.9 16.1 %collective-permute-start.3 = (f32[2,4,64,128]{3,2,1,0:T(8,128)S(1)}, f32[2,4,64,128]{3,2,1,0:T(8,128)S(1)}, u32[]{:S(2)}, u32[]{:S(2)}) collective-permute-start(f32[2,4,64,128]{3,2,1,0:T(8,128)S(1)} %dynamic-slice_bitcast_fusion.1.ready_ref), channel_id=1, source_target_pairs={{0,64},{64,0},{1,65},{65,1},{2,66},{66,2},{3,67},{67,3},{4,68},{68... | collective-permute-start | bytes 786440 | tf_op jit(solution)/shard_map/ppermute | solution.py:46
  100.0 3.7 %copy-start.2 = (f32[2048]{0:T(1024)S(1)}, f32[2048]{0:T(1024)}, u32[]{:S(2)}) copy-start(f32[2048]{0:T(1024)} %param.17) | copy-start | bytes 24580
  100.7 4.4 %collective-permute-start.4 = (f32[1024,128]{1,0:T(8,128)S(1)}, f32[1024,128]{1,0:T(8,128)S(1)}, u32[]{:S(2)}, u32[]{:S(2)}) collective-permute-start(f32[1024,128]{1,0:T(8,128)S(1)} %bitcast.31), channel_id=1, source_target_pairs={{0,16},{16,0},{1,17},{17,1},{2,18},{18,2},{3,19},{19,3},{4,20},{20... | collective-permute-start | bytes 1572872 | tf_op jit(solution)/shard_map/ppermute | solution.py:46

commit v3 on v2

--- a/solution.py
+++ b/solution.py
@@ -9,9 +9,9 @@
 SIZES = (2, 2, 2, 2, 2, 2, 2, 8)
 CODE = ("xh", "xm", "yh", "ym", "yl", "core")
 DP = ("xl", "z")
-NEAR = ("xm", "xl", "z")
+NEAR = ("xh", "xm", "z")
 TILE = 256
-FAR = ("xh", "yh", "ym", "yl")
+FAR = ("yh", "ym", "yl", "xl")
 
 
 def size(axes):
@@ -50,7 +50,8 @@
     return lax.dynamic_index_in_dim(value, place, axis, keepdims=False)
 
 
-def sum_kernel(first_ref, ids_ref, rows_ref, out_ref):
+def sum_kernel(first_ref, ids_ref, rows_ref, *refs):
+    arrived, (out_ref, token_ref) = refs[:-2], refs[-2:]
     width = rows_ref.shape[1]
     value = rows_ref[...]
     high = value.astype(jnp.bfloat16)
@@ -64,24 +65,23 @@
         hit = jnp.where(row == ids, 1.0, 0.0).astype(jnp.bfloat16)
         part = jnp.dot(hit, three, preferred_element_type=jnp.float32)
         total = part[:, :width] + part[:, width : 2 * width] + part[:, 2 * width :]
-        out_ref[tile * TILE : (tile + 1) * TILE, :] = total
-
-
-def partial_grad(ids, rows_grad, first, rows):
+        here = slice(tile * TILE, (tile + 1) * TILE)
+        out_ref[here, :] = total + arrived[0][here, :] if arrived else total
+    token_ref[...] = value[:8]
+
+
+def partial_grad(ids, rows_grad, first, rows, *arrived):
     lookups, width = rows_grad.shape
+    whole = pl.BlockSpec(memory_space=pltpu.VMEM)
     return pl.pallas_call(
         sum_kernel,
-        out_shape=jax.ShapeDtypeStruct((rows, width), jnp.float32),
-        in_specs=[
-            pl.BlockSpec(memory_space=pltpu.SMEM),
-            pl.BlockSpec(memory_space=pltpu.VMEM),
-            pl.BlockSpec(memory_space=pltpu.VMEM),
-        ],
-        out_specs=pl.BlockSpec(memory_space=pltpu.VMEM),
+        out_shape=[jax.ShapeDtypeStruct((rows, width), jnp.float32), jax.ShapeDtypeStruct((8, width), jnp.float32)],
+        in_specs=[pl.BlockSpec(memory_space=pltpu.SMEM), whole, whole] + [whole] * len(arrived),
+        out_specs=[whole, whole],
         cost_estimate=pl.CostEstimate(flops=6 * rows * lookups * width, bytes_accessed=4 * (lookups + rows) * width, transcendentals=0),
-        compiler_params=pltpu.CompilerParams(vmem_limit_bytes=24 << 20),
+        compiler_params=pltpu.CompilerParams(vmem_limit_bytes=(24 if arrived else 56) << 20),
         name="hot_rows_sum",
-    )(first.reshape(1), ids.reshape(1, lookups), rows_grad)
+    )(first.reshape(1), ids.reshape(1, lookups), rows_grad, *arrived)
 
 
 def coded_kernel(ids_ref, counts_ref, column_ref, core_ref, coef_ref, cold_ref, ready_ref, kept_ref, sent_ref):
@@ -163,11 +163,13 @@
     core = lax.axis_index("core")
 
     half = hot_rows // 2
-    theirs = partial_grad(batch_ids[0, 0], out_grad[0, 0], (1 - core) * half, half)
+    theirs, token = partial_grad(batch_ids[0, 0], out_grad[0, 0], (1 - core) * half, half)
     arrived = swap(theirs, "core")
 
+    grad, _ = partial_grad(batch_ids[0, 0], out_grad[0, 0], core * half, half, arrived)
+
     table = cold_table[0, 0].reshape(-1, 4, 2, part_rows, width)
-    parity, away = coded(table, block_ids[0, 0], counts[0], group_map, coef, core, theirs)
+    parity, away = coded(table, block_ids[0, 0], counts[0], group_map, coef, core, token)
     parity = parity + swap(away, "core")
     parity = parity.reshape(2, slot_count, 2, 2, part_rows, width)
     near_y, far_y = lax.axis_index("yl"), lax.axis_index("ym")
@@ -176,7 +178,6 @@
     send_far = pick(parity, 1 - far_y, 2)
     parity_shards = (pick(parity, far_y, 2) + swap(send_far, "ym"))[None, None]
 
-    grad = partial_grad(batch_ids[0, 0], out_grad[0, 0], core * half, half) + arrived
     near = size(NEAR)
     parts = exchange(grad.reshape(near, half // near, width), NEAR)
     parts = exchange(sum_copies(parts, size(FAR), send_near), FAR)

time: 107 us -> 107 us (level)
  Pallas kernels: 8.3 us -> 11 us
  other arithmetic: 4.06 us -> 2.17 us
  starting transfers between devices: 53.8 us -> 55.6 us
  local copies, waits for them, and re-layouts: 2.47 us -> 0.76 us
  waiting for transfers between devices: 35.7 us -> 34.6 us
    ppermute x5, starting transfers between devices: 27.4 us -> 32 us  [swap(): return lax.ppermute(value, axis, [(0, 1), (1, 0)])]
    all_to_all x3, starting transfers between devices: 26.4 us -> 23.7 us  [exchange(): return lax.all_to_all(parts, axes, 0, 0, tiled=True)]
    pallas_call x2, Pallas kernels: 2.54 us -> 5.27 us  [partial_grad(): pl.pallas_call(sum_kernel, out_shape=[jax.ShapeDtypeStruct((rows, width),...]
    add x1 -> x0, other arithmetic: 1.89 us -> none  [shards(): partial_grad(batch_ids[0, 0], out_grad[0, 0], core * half, half) + arrived]
    unnamed x16, local copies, waits for them, and re-layouts: 2.39 us -> 0.69 us
    ppermute x5, waiting for transfers between devices: 13.8 us -> 12.6 us  [swap(): return lax.ppermute(value, axis, [(0, 1), (1, 0)])]
  transfers between devices with their start and end apart: 8 -> 8, of which waited for: 5 -> 4; matrix products, arithmetic and copies ran while one was open for 4% -> 2% of each run, Pallas kernels for 3% -> 5%
where the time goes in v3:
time: 107 us; the launch traced here: 106 us
  starting transfers between devices  55.6 us (52%)
  waiting for transfers between devices  34.6 us (32%)
  Pallas kernels  11 us (10%)
  other arithmetic  2.17 us (2%)
  between operations  2.15 us (2%)
    ppermute x5, starting transfers between devices, swap(): return lax.ppermute(value, axis, [(0, 1), (1, 0)])  32 us
    all_to_all x3, starting transfers between devices, exchange(): return lax.all_to_all(parts, axes, 0, 0, tiled=True)  23.7 us
    all_to_all x3, waiting for transfers between devices, exchange(): return lax.all_to_all(parts, axes, 0, 0, tiled=True)  22.1 us
    ppermute x5, waiting for transfers between devices, swap(): return lax.ppermute(value, axis, [(0, 1), (1, 0)])  12.6 us
    pallas_call x2, Pallas kernels, partial_grad(): pl.pallas_call(sum_kernel, out_shape=[jax.ShapeDtypeStruct((rows, width),...  5.27 us
    pallas_call x2, Pallas kernels, adagrad_half(): pl.pallas_call(adagrad_kernel, grid_spec=pltpu.PrefetchScalarGridSpec(num...  2.61 us
  transfers between devices with their start and end apart: 8, of which 4 were waited for; matrix products, arithmetic and copies ran while one was open for 2% of the time, Pallas kernels for 5%

profile of v3, /device:TPU:1, one launch (start us, length us, event | category | flops | bytes accessed | tf_op | source)
XLA Modules:
  0.0 106.4 jit_solution(15264936802968468787)
XLA Ops:
  0.6 3.2 %hot_rows_sum.2 = (f32[1024,128]{1,0:T(8,128)}, f32[8,128]{1,0:T(8,128)}) custom-call(s32[1]{0:T(128)} %bitcast.3.first_ref, s32[1,1024]{1,0:T(1,128)} %bitcast.39, f32[1024,128]{1,0:T(8,128)} %bitcast.37), custom_call_target="tpu_custom_call" | custom-call | flops 805306368 | bytes 1048576 | tf_op jit(solution)/shard_map/hot_rows_sum/pallas_call | solution.py:76
  3.9 16.1 %collective-permute-start = (f32[1024,128]{1,0:T(8,128)}, f32[1024,128]{1,0:T(8,128)S(1)}, u32[]{:S(2)}, u32[]{:S(2)}) collective-permute-start(f32[1024,128]{1,0:T(8,128)} %get-tuple-element.14), channel_id=1, source_target_pairs={{0,16},{16,0},{1,17},{17,1},{2,18},{18,2},{3,19},{19,3},{4,20},{20... | collective-permute-start | bytes 1572872 | tf_op jit(solution)/shard_map/ppermute | solution.py:46
  21.2 0.0 copy-start.3
  21.2 0.0 copy-start.4
  21.2 0.0 copy-start.5
  21.3 0.6 copy-done.3
  21.9 0.0 copy-done.4
  21.9 1.5 %coded_blocks.1 = (f32[2,4,4,64,128]{4,3,2,1,0:T(8,128)S(1)}, f32[2,4,4,64,128]{4,3,2,1,0:T(8,128)S(1)}) custom-call(s32[4]{0:T(128)S(1)} %bitcast.36, s32[1]{0:T(128)} %bitcast.30.counts_ref, s32[1]{0:T(128)S(6)} %copy.21.column_ref, s32[1]{0:T(128)} %bitcast.7.core_ref.place_ref, f32[2,8]{1,0:T(2,128)S(1)} %copy-done.4, ...), custom_call_target="tpu_custom_call" | custom-call | flops 786432 | bytes 3145728 | tf_op jit(solution)/shard_map/coded_blocks/pallas_call | solution.py:101
  23.4 0.0 copy-start.7
  23.4 1.9 %collective-permute-start.1 = (f32[2,4,4,64,128]{4,3,2,1,0:T(8,128)S(1)}, f32[2,4,4,64,128]{4,3,2,1,0:T(8,128)}, u32[]{:S(2)}, u32[]{:S(2)}) collective-permute-start(f32[2,4,4,64,128]{4,3,2,1,0:T(8,128)S(1)} %get-tuple-element.18), channel_id=1, source_target_pairs={{0,16},{16,0},{1,17},{17,1},{2,18},{18,2},{3,19},{19,3},{4,20},{20... | collective-permute-start | bytes 3145736 | tf_op jit(solution)/shard_map/ppermute | solution.py:46
  25.4 0.0 collective-permute-done.refs_0_
  25.4 2.1 %hot_rows_sum.3 = (f32[1024,128]{1,0:T(8,128)}, f32[8,128]{1,0:T(8,128)}) custom-call(s32[1]{0:T(128)} %bitcast.first_ref, s32[1,1024]{1,0:T(1,128)S(1)} %bitcast.40, f32[1024,128]{1,0:T(8,128)S(1)} %bitcast.38, f32[1024,128]{1,0:T(8,128)S(1)} %collective-permute-done.refs_0_), custom_call_target="tpu_custom_call" | custom-call | flops 805306368 | bytes 1048576 | tf_op jit(solution)/shard_map/hot_rows_sum/pallas_call | solution.py:76
  27.5 9.1 %all-to-all-start = ((f32[32,32,128]{2,1,0:T(8,128)}), f32[32,32,128]{2,1,0:T(8,128)S(1)}, u32[]{:S(2)}, u32[]{:S(2)}) async-start(f32[32,32,128]{2,1,0:T(8,128)} %bitcast.4), calls=%async_computation | async-start | bytes 1048576 | tf_op jit(solution)/shard_map/all_to_all | solution.py:22
  36.6 0.0 collective-permute-done.1
  36.6 1.4 %add.25 = f32[2,4,4,64,128]{4,3,2,1,0:T(8,128)S(1)} add(f32[2,4,4,64,128]{4,3,2,1,0:T(8,128)S(1)} %get-tuple-element.17, f32[2,4,4,64,128]{4,3,2,1,0:T(8,128)} %collective-permute-done.1) | non-fusion elementwise | flops 262144 | bytes 3145728 | tf_op jit(solution)/shard_map/add | solution.py:173
  37.9 0.1 dynamic-slice_bitcast_fusion.ready_ref
  38.0 3.3 %collective-permute-start.2 = (f32[2,4,2,64,128]{4,3,2,1,0:T(8,128)S(1)}, f32[2,4,2,64,128]{4,3,2,1,0:T(8,128)S(1)}, u32[]{:S(2)}, u32[]{:S(2)}) collective-permute-start(f32[2,4,2,64,128]{4,3,2,1,0:T(8,128)S(1)} %dynamic-slice_bitcast_fusion.ready_ref), channel_id=1, source_target_pairs={{0,32},{32,0},{1,33},{33,1},{2,34},{34,2},{3,35},{35,3},{4,36},{36... | collective-permute-start | bytes 1572872 | tf_op jit(solution)/shard_map/ppermute | solution.py:46
  41.3 13.3 %all-to-all-done.parts_ref = f32[32,32,128]{2,1,0:T(8,128)S(1)} async-done(((f32[32,32,128]{2,1,0:T(8,128)}), f32[32,32,128]{2,1,0:T(8,128)S(1)}, u32[]{:S(2)}, u32[]{:S(2)}) %all-to-all-start) | async-done | bytes 524320 | tf_op jit(solution)/shard_map/all_to_all | solution.py:22
  54.7 0.8 sum_copies.2
  55.4 7.3 %all-to-all-start.1 = ((f32[16,32,128]{2,1,0:T(8,128)}), f32[16,32,128]{2,1,0:T(8,128)S(1)}, u32[]{:S(2)}, u32[]{:S(2)}) async-start(f32[16,32,128]{2,1,0:T(8,128)} %sum_copies.2), calls=%async_computation.1 | async-start | bytes 524288 | tf_op jit(solution)/shard_map/all_to_all | solution.py:22
  62.8 0.0 collective-permute-done.2
  62.8 0.1 bitcast_add_fusion
  62.9 8.7 %all-to-all-done.1.parts_ref = f32[16,32,128]{2,1,0:T(8,128)S(1)} async-done(((f32[16,32,128]{2,1,0:T(8,128)}), f32[16,32,128]{2,1,0:T(8,128)S(1)}, u32[]{:S(2)}, u32[]{:S(2)}) %all-to-all-start.1) | async-done | bytes 262176 | tf_op jit(solution)/shard_map/all_to_all | solution.py:22
  71.6 0.9 sum_copies.3
  72.5 7.3 %all-to-all-start.2 = ((f32[32,32,128]{2,1,0:T(8,128)}), f32[32,32,128]{2,1,0:T(8,128)S(1)}, u32[]{:S(2)}, u32[]{:S(2)}) async-start(f32[32,32,128]{2,1,0:T(8,128)} %sum_copies.3), calls=%async_computation.2 | async-start | bytes 1048576 | tf_op jit(solution)/shard_map/all_to_all | solution.py:22
  79.8 2.5 %collective-permute-start.3 = (f32[2,4,64,128]{3,2,1,0:T(8,128)S(1)}, f32[2,4,64,128]{3,2,1,0:T(8,128)S(1)}, u32[]{:S(2)}, u32[]{:S(2)}) collective-permute-start(f32[2,4,64,128]{3,2,1,0:T(8,128)S(1)} %dynamic-slice_bitcast_fusion.1.ready_ref), channel_id=1, source_target_pairs={{0,64},{64,0},{1,65},{65,1},{2,66},{66,2},{3,67},{67,3},{4,68},{68... | collective-permute-start | bytes 786440 | tf_op jit(solution)/shard_map/ppermute | solution.py:46
  82.2 12.4 %collective-permute-done.3 = f32[2,4,64,128]{3,2,1,0:T(8,128)S(1)} collective-permute-done((f32[2,4,64,128]{3,2,1,0:T(8,128)S(1)}, f32[2,4,64,128]{3,2,1,0:T(8,128)S(1)}, u32[]{:S(2)}, u32[]{:S(2)}) %collective-permute-start.3) | collective-permute-done | bytes 262176 | tf_op jit(solution)/shard_map/ppermute | solution.py:46
  94.6 0.7 fusion
  95.3 8.2 %collective-permute-start.4 = (f32[1024,128]{1,0:T(8,128)S(1)}, f32[1024,128]{1,0:T(8,128)S(1)}, u32[]{:S(2)}, u32[]{:S(2)}) collective-permute-start(f32[1024,128]{1,0:T(8,128)S(1)} %bitcast.31), channel_id=1, source_target_pairs={{0,16},{16,0},{1,17},{17,1},{2,18},{18,2},{3,19},{19,3},{4,20},{20... | collective-permute-start | bytes 1572872 | tf_op jit(solution)/shard_map/ppermute | solution.py:46
  103.6 1.3 %hot_rows_adagrad.2 = (f32[2048,128]{1,0:T(8,128)}, f32[16,128]{1,0:T(8,128)}) custom-call(s32[1]{0:T(128)} %bitcast.7.core_ref.place_ref, f32[1024,128]{1,0:T(8,128)S(1)} %bitcast.32, f32[2048,128]{1,0:T(8,128)S(1)} %copy-done, f32[16,128]{1,0:T(8,128)S(1)} %bitcast.34), custom_call_target="tpu_custom_call" | custom-call | flops 1048576 | bytes 1572864 | tf_op jit(solution)/shard_map/hot_rows_adagrad/pallas_call | solution.py:136
  104.9 0.2 collective-permute-done.4.grad_ref
  105.1 1.3 %hot_rows_adagrad.3 = (f32[2048,128]{1,0:T(8,128)}, f32[16,128]{1,0:T(8,128)}) custom-call(s32[1]{0:T(128)} %bitcast.16.place_ref, f32[1024,128]{1,0:T(8,128)S(1)} %collective-permute-done.4.grad_ref, f32[2048,128]{1,0:T(8,128)S(1)} %copy-done, f32[16,128]{1,0:T(8,128)S(1)} %bitcast.35, ...), custom_call_target="tpu_custom_call", output_to_operand_aliasing={{0}: (4, {}), {1}: (5, {})} | custom-call | flops 1048576 | bytes 1572864 | tf_op jit(solution)/shard_map/hot_rows_adagrad/pallas_call | solution.py:136
  (12 shorter events, 0.0 us)
Async XLA Ops:
  0.6 20.6 %copy-start.1 = (f32[1,1,4,512,128]{4,3,2,1,0:T(8,128)S(1)}, f32[1,1,4,512,128]{4,3,2,1,0:T(8,128)}, u32[]{:S(2)}) copy-start(f32[1,1,4,512,128]{4,3,2,1,0:T(8,128)} %param.9) | copy-start | bytes 3145732
  3.9 21.5 %collective-permute-start = (f32[1024,128]{1,0:T(8,128)}, f32[1024,128]{1,0:T(8,128)S(1)}, u32[]{:S(2)}, u32[]{:S(2)}) collective-permute-start(f32[1024,128]{1,0:T(8,128)} %get-tuple-element.14), channel_id=1, source_target_pairs={{0,16},{16,0},{1,17},{17,1},{2,18},{18,2},{3,19},{19,3},{4,20},{20... | collective-permute-start | bytes 1572872 | tf_op jit(solution)/shard_map/ppermute | solution.py:46
  21.2 0.7 copy-start.3
  21.2 0.7 copy-start.4
  21.2 0.7 copy-start.5
  21.9 3.5 %copy-start.6 = (f32[1,1,1024,128]{3,2,1,0:T(8,128)S(1)}, f32[1,1,1024,128]{3,2,1,0:T(8,128)}, u32[]{:S(2)}) copy-start(f32[1,1,1024,128]{3,2,1,0:T(8,128)} %param.15) | copy-start | bytes 1572868
  23.4 2.0 %copy-start.7 = (s32[1,1,1024]{2,1,0:T(1,128)S(1)}, s32[1,1,1024]{2,1,0:T(1,128)}, u32[]{:S(2)}) copy-start(s32[1,1,1024]{2,1,0:T(1,128)} %param.14) | copy-start | bytes 12292
  23.4 13.1 %collective-permute-start.1 = (f32[2,4,4,64,128]{4,3,2,1,0:T(8,128)S(1)}, f32[2,4,4,64,128]{4,3,2,1,0:T(8,128)}, u32[]{:S(2)}, u32[]{:S(2)}) collective-permute-start(f32[2,4,4,64,128]{4,3,2,1,0:T(8,128)S(1)} %get-tuple-element.18), channel_id=1, source_target_pairs={{0,16},{16,0},{1,17},{17,1},{2,18},{18,2},{3,19},{19,3},{4,20},{20... | collective-permute-start | bytes 3145736 | tf_op jit(solution)/shard_map/ppermute | solution.py:46
  27.5 27.2 %all-to-all-start = ((f32[32,32,128]{2,1,0:T(8,128)}), f32[32,32,128]{2,1,0:T(8,128)S(1)}, u32[]{:S(2)}, u32[]{:S(2)}) async-start(f32[32,32,128]{2,1,0:T(8,128)} %bitcast.4), calls=%async_computation | async-start | bytes 1048576 | tf_op jit(solution)/shard_map/all_to_all | solution.py:22
  38.0 24.8 %collective-permute-start.2 = (f32[2,4,2,64,128]{4,3,2,1,0:T(8,128)S(1)}, f32[2,4,2,64,128]{4,3,2,1,0:T(8,128)S(1)}, u32[]{:S(2)}, u32[]{:S(2)}) collective-permute-start(f32[2,4,2,64,128]{4,3,2,1,0:T(8,128)S(1)} %dynamic-slice_bitcast_fusion.ready_ref), channel_id=1, source_target_pairs={{0,32},{32,0},{1,33},{33,1},{2,34},{34,2},{3,35},{35,3},{4,36},{36... | collective-permute-start | bytes 1572872 | tf_op jit(solution)/shard_map/ppermute | solution.py:46
  55.4 16.2 %all-to-all-start.1 = ((f32[16,32,128]{2,1,0:T(8,128)}), f32[16,32,128]{2,1,0:T(8,128)S(1)}, u32[]{:S(2)}, u32[]{:S(2)}) async-start(f32[16,32,128]{2,1,0:T(8,128)} %sum_copies.2), calls=%async_computation.1 | async-start | bytes 524288 | tf_op jit(solution)/shard_map/all_to_all | solution.py:22
  72.5 31.1 %copy-start = (f32[2048,128]{1,0:T(8,128)S(1)}, f32[2048,128]{1,0:T(8,128)}, u32[]{:S(2)}) copy-start(f32[2048,128]{1,0:T(8,128)} %weights_ref.3) | copy-start | bytes 3145732
  72.5 22.8 %all-to-all-start.2 = ((f32[32,32,128]{2,1,0:T(8,128)}), f32[32,32,128]{2,1,0:T(8,128)S(1)}, u32[]{:S(2)}, u32[]{:S(2)}) async-start(f32[32,32,128]{2,1,0:T(8,128)} %sum_copies.3), calls=%async_computation.2 | async-start | bytes 1048576 | tf_op jit(solution)/shard_map/all_to_all | solution.py:22
  79.8 14.8 %collective-permute-start.3 = (f32[2,4,64,128]{3,2,1,0:T(8,128)S(1)}, f32[2,4,64,128]{3,2,1,0:T(8,128)S(1)}, u32[]{:S(2)}, u32[]{:S(2)}) collective-permute-start(f32[2,4,64,128]{3,2,1,0:T(8,128)S(1)} %dynamic-slice_bitcast_fusion.1.ready_ref), channel_id=1, source_target_pairs={{0,64},{64,0},{1,65},{65,1},{2,66},{66,2},{3,67},{67,3},{4,68},{68... | collective-permute-start | bytes 786440 | tf_op jit(solution)/shard_map/ppermute | solution.py:46
  94.6 9.0 %copy-start.2 = (f32[2048]{0:T(1024)S(1)}, f32[2048]{0:T(1024)}, u32[]{:S(2)}) copy-start(f32[2048]{0:T(1024)} %param.17) | copy-start | bytes 24580
  95.3 9.7 %collective-permute-start.4 = (f32[1024,128]{1,0:T(8,128)S(1)}, f32[1024,128]{1,0:T(8,128)S(1)}, u32[]{:S(2)}, u32[]{:S(2)}) collective-permute-start(f32[1024,128]{1,0:T(8,128)S(1)} %bitcast.31), channel_id=1, source_target_pairs={{0,16},{16,0},{1,17},{17,1},{2,18},{18,2},{3,19},{19,3},{4,20},{20... | collective-permute-start | bytes 1572872 | tf_op jit(solution)/shard_map/ppermute | solution.py:46

commit v4 on v3

--- a/solution.py
+++ b/solution.py
@@ -9,9 +9,9 @@
 SIZES = (2, 2, 2, 2, 2, 2, 2, 8)
 CODE = ("xh", "xm", "yh", "ym", "yl", "core")
 DP = ("xl", "z")
-NEAR = ("xh", "xm", "z")
+NEAR = ("yl", "xl", "z")
 TILE = 256
-FAR = ("yh", "ym", "yl", "xl")
+FAR = ("xh", "xm", "yh", "ym")
 
 
 def size(axes):
@@ -51,7 +51,7 @@
 
 
 def sum_kernel(first_ref, ids_ref, rows_ref, *refs):
-    arrived, (out_ref, token_ref) = refs[:-2], refs[-2:]
+    arrived, out_ref = refs[:-1], refs[-1]
     width = rows_ref.shape[1]
     value = rows_ref[...]
     high = value.astype(jnp.bfloat16)
@@ -67,7 +67,6 @@
         total = part[:, :width] + part[:, width : 2 * width] + part[:, 2 * width :]
         here = slice(tile * TILE, (tile + 1) * TILE)
         out_ref[here, :] = total + arrived[0][here, :] if arrived else total
-    token_ref[...] = value[:8]
 
 
 def partial_grad(ids, rows_grad, first, rows, *arrived):
@@ -75,26 +74,26 @@
     whole = pl.BlockSpec(memory_space=pltpu.VMEM)
     return pl.pallas_call(
         sum_kernel,
-        out_shape=[jax.ShapeDtypeStruct((rows, width), jnp.float32), jax.ShapeDtypeStruct((8, width), jnp.float32)],
+        out_shape=jax.ShapeDtypeStruct((rows, width), jnp.float32),
         in_specs=[pl.BlockSpec(memory_space=pltpu.SMEM), whole, whole] + [whole] * len(arrived),
-        out_specs=[whole, whole],
+        out_specs=whole,
         cost_estimate=pl.CostEstimate(flops=6 * rows * lookups * width, bytes_accessed=4 * (lookups + rows) * width, transcendentals=0),
         compiler_params=pltpu.CompilerParams(vmem_limit_bytes=(24 if arrived else 56) << 20),
         name="hot_rows_sum",
     )(first.reshape(1), ids.reshape(1, lookups), rows_grad, *arrived)
 
 
-def coded_kernel(ids_ref, counts_ref, column_ref, core_ref, coef_ref, cold_ref, ready_ref, kept_ref, sent_ref):
+def coded_kernel(ids_ref, counts_ref, column_ref, core_ref, coef_ref, cold_ref, kept_ref, sent_ref):
     slot, core, column = pl.program_id(0), core_ref[0], column_ref[0]
-    live = jnp.where(slot < counts_ref[0], 1.0, 0.0)
+    live = jnp.where(slot < counts_ref[0, 0], 1.0, 0.0)
     kept, sent = cold_ref[0, :, core] * live, cold_ref[0, :, 1 - core] * live
     for parity in range(kept_ref.shape[0]):
         kept_ref[parity, 0] = coef_ref[parity, column] * kept
         sent_ref[parity, 0] = coef_ref[parity, column] * sent
 
 
-def coded(cold_table, block_ids, counts, group_map, coef, core, ready):
-    parities, slots = coef.shape[0], block_ids.shape[0]
+def coded(cold_table, block_ids, counts, group_map, coef, core):
+    parities, slots = coef.shape[0], block_ids.shape[2]
     rest = cold_table.shape[1:]
     shape = (parities, slots, rest[0]) + rest[2:]
     out = pl.BlockSpec((parities, 1) + shape[2:], lambda s, *refs: (0, s, 0, 0, 0))
@@ -105,8 +104,7 @@
             grid=(slots,),
             in_specs=[
                 pl.BlockSpec(memory_space=pltpu.SMEM),
-                pl.BlockSpec((1,) + rest, lambda s, ids, *refs: (ids[s], 0, 0, 0, 0)),
-                pl.BlockSpec(memory_space=pl.ANY),
+                pl.BlockSpec((1,) + rest, lambda s, ids, *refs: (ids[0, 0, s], 0, 0, 0, 0)),
             ],
             out_specs=[out, out],
         ),
@@ -114,7 +112,7 @@
         cost_estimate=pl.CostEstimate(flops=cold_table.size * 3, bytes_accessed=12 * cold_table.size, transcendentals=0),
         compiler_params=pltpu.CompilerParams(vmem_limit_bytes=24 << 20),
         name="coded_blocks",
-    )(block_ids, counts, group_map, core.reshape(1), coef, cold_table, ready)
+    )(block_ids, counts, group_map, core.reshape(1), coef, cold_table)
 
 
 def adagrad_kernel(place_ref, grad_ref, weights_ref, accum_ref, *refs):
@@ -163,13 +161,14 @@
     core = lax.axis_index("core")
 
     half = hot_rows // 2
-    theirs, token = partial_grad(batch_ids[0, 0], out_grad[0, 0], (1 - core) * half, half)
+    theirs = partial_grad(batch_ids[0, 0], out_grad[0, 0], (1 - core) * half, half)
     arrived = swap(theirs, "core")
 
-    grad, _ = partial_grad(batch_ids[0, 0], out_grad[0, 0], core * half, half, arrived)
-
+    grad = partial_grad(batch_ids[0, 0], out_grad[0, 0], core * half, half, arrived)
+
+    cold_table, theirs = lax.optimization_barrier((cold_table, theirs))
     table = cold_table[0, 0].reshape(-1, 4, 2, part_rows, width)
-    parity, away = coded(table, block_ids[0, 0], counts[0], group_map, coef, core, token)
+    parity, away = coded(table, block_ids, counts, group_map, coef, core)
     parity = parity + swap(away, "core")
     parity = parity.reshape(2, slot_count, 2, 2, part_rows, width)
     near_y, far_y = lax.axis_index("yl"), lax.axis_index("ym")

time: 107 us -> 106 us (level)
  starting transfers between devices: 55.6 us -> 52.3 us
  waiting for transfers between devices: 34.6 us -> 36.7 us
    ppermute x5, starting transfers between devices: 32 us -> 27.2 us  [swap(): return lax.ppermute(value, axis, [(0, 1), (1, 0)])]
    all_to_all x3, starting transfers between devices: 23.7 us -> 25.1 us  [exchange(): return lax.all_to_all(parts, axes, 0, 0, tiled=True)]
    all_to_all x3, waiting for transfers between devices: 22.1 us -> 23.3 us  [exchange(): return lax.all_to_all(parts, axes, 0, 0, tiled=True)]
where the time goes in v4:
time: 106 us; the launch traced here: 105 us
  starting transfers between devices  52.3 us (49%)
  waiting for transfers between devices  36.7 us (35%)
  Pallas kernels  11 us (10%)
  other arithmetic  2.17 us (2%)
  between operations  2.14 us (2%)
    ppermute x5, starting transfers between devices, swap(): return lax.ppermute(value, axis, [(0, 1), (1, 0)])  27.2 us
    all_to_all x3, starting transfers between devices, exchange(): return lax.all_to_all(parts, axes, 0, 0, tiled=True)  25.1 us
    all_to_all x3, waiting for transfers between devices, exchange(): return lax.all_to_all(parts, axes, 0, 0, tiled=True)  23.3 us
    ppermute x5, waiting for transfers between devices, swap(): return lax.ppermute(value, axis, [(0, 1), (1, 0)])  13.4 us
    pallas_call x2, Pallas kernels, partial_grad(): pl.pallas_call(sum_kernel, out_shape=jax.ShapeDtypeStruct((rows, width),...  5.27 us
    pallas_call x2, Pallas kernels, adagrad_half(): pl.pallas_call(adagrad_kernel, grid_spec=pltpu.PrefetchScalarGridSpec(num...  2.61 us
  transfers between devices with their start and end apart: 8, of which 4 were waited for; matrix products, arithmetic and copies ran while one was open for 2% of the time, Pallas kernels for 5%

profile of v4, /device:TPU:1, one launch (start us, length us, event | category | flops | bytes accessed | tf_op | source)
XLA Modules:
  0.0 105.1 jit_solution(8477398607238741258)
XLA Ops:
  0.6 0.0 copy-start.1
  0.6 3.2 %hot_rows_sum.2 = f32[1024,128]{1,0:T(8,128)} custom-call(s32[1]{0:T(128)} %bitcast.3.first_ref, s32[1,1024]{1,0:T(1,128)} %bitcast.35, f32[1024,128]{1,0:T(8,128)} %bitcast.33), custom_call_target="tpu_custom_call" | custom-call | flops 805306368 | bytes 1048576 | tf_op jit(solution)/shard_map/hot_rows_sum/pallas_call | solution.py:75
  3.9 16.1 %collective-permute-start = (f32[1024,128]{1,0:T(8,128)}, f32[1024,128]{1,0:T(8,128)S(1)}, u32[]{:S(2)}, u32[]{:S(2)}) collective-permute-start(f32[1024,128]{1,0:T(8,128)} %hot_rows_sum.2), channel_id=1, source_target_pairs={{0,16},{16,0},{1,17},{17,1},{2,18},{18,2},{3,19},{19,3},{4,20},{20... | collective-permute-start | bytes 1572872 | tf_op jit(solution)/shard_map/ppermute | solution.py:46
  21.2 0.0 copy-start.3
  21.2 0.0 copy-start.4
  21.2 0.6 copy-done.3
  21.9 1.5 %coded_blocks.1 = (f32[2,4,4,64,128]{4,3,2,1,0:T(8,128)S(1)}, f32[2,4,4,64,128]{4,3,2,1,0:T(8,128)S(1)}) custom-call(s32[1,1,4]{2,1,0:T(1,128)S(1)} %copy-done.4, s32[1,1]{1,0:T(1,128)S(6)} %copy.20.counts_ref, s32[1]{0:T(128)S(6)} %copy.21.column_ref, s32[1]{0:T(128)} %bitcast.5.core_ref.place_ref, f32[2,8]{1,0:T(2,128)S(1)} %copy-done.3, ...), custom_call_target="tpu_custom_call" | custom-call | flops 786432 | bytes 3145728 | tf_op jit(solution)/shard_map/coded_blocks/pallas_call | solution.py:100
  23.4 0.0 copy-start.6
  23.4 1.9 %collective-permute-start.1 = (f32[2,4,4,64,128]{4,3,2,1,0:T(8,128)S(1)}, f32[2,4,4,64,128]{4,3,2,1,0:T(8,128)}, u32[]{:S(2)}, u32[]{:S(2)}) collective-permute-start(f32[2,4,4,64,128]{4,3,2,1,0:T(8,128)S(1)} %get-tuple-element.14), channel_id=1, source_target_pairs={{0,16},{16,0},{1,17},{17,1},{2,18},{18,2},{3,19},{19,3},{4,20},{20... | collective-permute-start | bytes 3145736 | tf_op jit(solution)/shard_map/ppermute | solution.py:46
  25.4 0.0 collective-permute-done.refs_0_
  25.4 2.1 %hot_rows_sum.3 = f32[1024,128]{1,0:T(8,128)} custom-call(s32[1]{0:T(128)} %bitcast.first_ref, s32[1,1024]{1,0:T(1,128)S(1)} %bitcast.36, f32[1024,128]{1,0:T(8,128)S(1)} %bitcast.34, f32[1024,128]{1,0:T(8,128)S(1)} %collective-permute-done.refs_0_), custom_call_target="tpu_custom_call" | custom-call | flops 805306368 | bytes 1048576 | tf_op jit(solution)/shard_map/hot_rows_sum/pallas_call | solution.py:75
  27.5 6.2 %all-to-all-start = ((f32[32,32,128]{2,1,0:T(8,128)}), f32[32,32,128]{2,1,0:T(8,128)S(1)}, u32[]{:S(2)}, u32[]{:S(2)}) async-start(f32[32,32,128]{2,1,0:T(8,128)} %bitcast.4), calls=%async_computation | async-start | bytes 1048576 | tf_op jit(solution)/shard_map/all_to_all | solution.py:22
  33.7 0.0 collective-permute-done.1
  33.7 1.4 %add.25 = f32[2,4,4,64,128]{4,3,2,1,0:T(8,128)S(1)} add(f32[2,4,4,64,128]{4,3,2,1,0:T(8,128)S(1)} %get-tuple-element.13, f32[2,4,4,64,128]{4,3,2,1,0:T(8,128)} %collective-permute-done.1) | non-fusion elementwise | flops 262144 | bytes 3145728 | tf_op jit(solution)/shard_map/add | solution.py:172
  35.0 0.1 dynamic-slice_bitcast_fusion.ready_ref
  35.1 3.1 %collective-permute-start.2 = (f32[2,4,2,64,128]{4,3,2,1,0:T(8,128)S(1)}, f32[2,4,2,64,128]{4,3,2,1,0:T(8,128)S(1)}, u32[]{:S(2)}, u32[]{:S(2)}) collective-permute-start(f32[2,4,2,64,128]{4,3,2,1,0:T(8,128)S(1)} %dynamic-slice_bitcast_fusion.ready_ref), channel_id=1, source_target_pairs={{0,32},{32,0},{1,33},{33,1},{2,34},{34,2},{3,35},{35,3},{4,36},{36... | collective-permute-start | bytes 1572872 | tf_op jit(solution)/shard_map/ppermute | solution.py:46
  38.3 11.6 %all-to-all-done.parts_ref = f32[32,32,128]{2,1,0:T(8,128)S(1)} async-done(((f32[32,32,128]{2,1,0:T(8,128)}), f32[32,32,128]{2,1,0:T(8,128)S(1)}, u32[]{:S(2)}, u32[]{:S(2)}) %all-to-all-start) | async-done | bytes 524320 | tf_op jit(solution)/shard_map/all_to_all | solution.py:22
  49.8 0.8 sum_copies.2
  50.6 10.5 %all-to-all-start.1 = ((f32[16,32,128]{2,1,0:T(8,128)}), f32[16,32,128]{2,1,0:T(8,128)S(1)}, u32[]{:S(2)}, u32[]{:S(2)}) async-start(f32[16,32,128]{2,1,0:T(8,128)} %sum_copies.2), calls=%async_computation.1 | async-start | bytes 524288 | tf_op jit(solution)/shard_map/all_to_all | solution.py:22
  61.1 0.0 collective-permute-done.2
  61.1 0.1 bitcast_add_fusion
  61.2 11.7 %all-to-all-done.1.parts_ref = f32[16,32,128]{2,1,0:T(8,128)S(1)} async-done(((f32[16,32,128]{2,1,0:T(8,128)}), f32[16,32,128]{2,1,0:T(8,128)S(1)}, u32[]{:S(2)}, u32[]{:S(2)}) %all-to-all-start.1) | async-done | bytes 262176 | tf_op jit(solution)/shard_map/all_to_all | solution.py:22
  72.9 0.9 sum_copies.3
  73.8 8.4 %all-to-all-start.2 = ((f32[32,32,128]{2,1,0:T(8,128)}), f32[32,32,128]{2,1,0:T(8,128)S(1)}, u32[]{:S(2)}, u32[]{:S(2)}) async-start(f32[32,32,128]{2,1,0:T(8,128)} %sum_copies.3), calls=%async_computation.2 | async-start | bytes 1048576 | tf_op jit(solution)/shard_map/all_to_all | solution.py:22
  82.2 2.5 %collective-permute-start.3 = (f32[2,4,64,128]{3,2,1,0:T(8,128)S(1)}, f32[2,4,64,128]{3,2,1,0:T(8,128)S(1)}, u32[]{:S(2)}, u32[]{:S(2)}) collective-permute-start(f32[2,4,64,128]{3,2,1,0:T(8,128)S(1)} %dynamic-slice_bitcast_fusion.1.ready_ref), channel_id=1, source_target_pairs={{0,64},{64,0},{1,65},{65,1},{2,66},{66,2},{3,67},{67,3},{4,68},{68... | collective-permute-start | bytes 786440 | tf_op jit(solution)/shard_map/ppermute | solution.py:46
  84.7 13.2 %collective-permute-done.3 = f32[2,4,64,128]{3,2,1,0:T(8,128)S(1)} collective-permute-done((f32[2,4,64,128]{3,2,1,0:T(8,128)S(1)}, f32[2,4,64,128]{3,2,1,0:T(8,128)S(1)}, u32[]{:S(2)}, u32[]{:S(2)}) %collective-permute-start.3) | collective-permute-done | bytes 262176 | tf_op jit(solution)/shard_map/ppermute | solution.py:46
  98.0 0.7 fusion
  98.7 0.0 all-to-all-done.2
  98.7 3.6 %collective-permute-start.4 = (f32[1024,128]{1,0:T(8,128)S(1)}, f32[1024,128]{1,0:T(8,128)S(1)}, u32[]{:S(2)}, u32[]{:S(2)}) collective-permute-start(f32[1024,128]{1,0:T(8,128)S(1)} %bitcast.28), channel_id=1, source_target_pairs={{0,16},{16,0},{1,17},{17,1},{2,18},{18,2},{3,19},{19,3},{4,20},{20... | collective-permute-start | bytes 1572872 | tf_op jit(solution)/shard_map/ppermute | solution.py:46
  102.3 1.3 %hot_rows_adagrad.2 = (f32[2048,128]{1,0:T(8,128)}, f32[16,128]{1,0:T(8,128)}) custom-call(s32[1]{0:T(128)} %bitcast.5.core_ref.place_ref, f32[1024,128]{1,0:T(8,128)S(1)} %bitcast.29, f32[2048,128]{1,0:T(8,128)S(1)} %copy-done, f32[16,128]{1,0:T(8,128)S(1)} %bitcast.31), custom_call_target="tpu_custom_call" | custom-call | flops 1048576 | bytes 1572864 | tf_op jit(solution)/shard_map/hot_rows_adagrad/pallas_call | solution.py:134
  103.6 0.2 collective-permute-done.4.grad_ref
  103.8 1.3 %hot_rows_adagrad.3 = (f32[2048,128]{1,0:T(8,128)}, f32[16,128]{1,0:T(8,128)}) custom-call(s32[1]{0:T(128)} %bitcast.14.place_ref, f32[1024,128]{1,0:T(8,128)S(1)} %collective-permute-done.4.grad_ref, f32[2048,128]{1,0:T(8,128)S(1)} %copy-done, f32[16,128]{1,0:T(8,128)S(1)} %bitcast.32, ...), custom_call_target="tpu_custom_call", output_to_operand_aliasing={{0}: (4, {}), {1}: (5, {})} | custom-call | flops 1048576 | bytes 1572864 | tf_op jit(solution)/shard_map/hot_rows_adagrad/pallas_call | solution.py:134
  (10 shorter events, 0.0 us)
Async XLA Ops:
  0.6 20.6 %copy-start.1 = (f32[1,1,4,512,128]{4,3,2,1,0:T(8,128)S(1)}, f32[1,1,4,512,128]{4,3,2,1,0:T(8,128)}, u32[]{:S(2)}) copy-start(f32[1,1,4,512,128]{4,3,2,1,0:T(8,128)} %param.9) | copy-start | bytes 3145732
  3.9 21.5 %collective-permute-start = (f32[1024,128]{1,0:T(8,128)}, f32[1024,128]{1,0:T(8,128)S(1)}, u32[]{:S(2)}, u32[]{:S(2)}) collective-permute-start(f32[1024,128]{1,0:T(8,128)} %hot_rows_sum.2), channel_id=1, source_target_pairs={{0,16},{16,0},{1,17},{17,1},{2,18},{18,2},{3,19},{19,3},{4,20},{20... | collective-permute-start | bytes 1572872 | tf_op jit(solution)/shard_map/ppermute | solution.py:46
  21.2 0.7 copy-start.3
  21.2 0.7 copy-start.4
  21.9 3.5 %copy-start.5 = (f32[1,1,1024,128]{3,2,1,0:T(8,128)S(1)}, f32[1,1,1024,128]{3,2,1,0:T(8,128)}, u32[]{:S(2)}) copy-start(f32[1,1,1024,128]{3,2,1,0:T(8,128)} %param.15) | copy-start | bytes 1572868
  23.4 2.0 %copy-start.6 = (s32[1,1,1024]{2,1,0:T(1,128)S(1)}, s32[1,1,1024]{2,1,0:T(1,128)}, u32[]{:S(2)}) copy-start(s32[1,1,1024]{2,1,0:T(1,128)} %param.14) | copy-start | bytes 12292
  23.4 10.2 %collective-permute-start.1 = (f32[2,4,4,64,128]{4,3,2,1,0:T(8,128)S(1)}, f32[2,4,4,64,128]{4,3,2,1,0:T(8,128)}, u32[]{:S(2)}, u32[]{:S(2)}) collective-permute-start(f32[2,4,4,64,128]{4,3,2,1,0:T(8,128)S(1)} %get-tuple-element.14), channel_id=1, source_target_pairs={{0,16},{16,0},{1,17},{17,1},{2,18},{18,2},{3,19},{19,3},{4,20},{20... | collective-permute-start | bytes 3145736 | tf_op jit(solution)/shard_map/ppermute | solution.py:46
  27.5 22.4 %all-to-all-start = ((f32[32,32,128]{2,1,0:T(8,128)}), f32[32,32,128]{2,1,0:T(8,128)S(1)}, u32[]{:S(2)}, u32[]{:S(2)}) async-start(f32[32,32,128]{2,1,0:T(8,128)} %bitcast.4), calls=%async_computation | async-start | bytes 1048576 | tf_op jit(solution)/shard_map/all_to_all | solution.py:22
  35.1 26.0 %collective-permute-start.2 = (f32[2,4,2,64,128]{4,3,2,1,0:T(8,128)S(1)}, f32[2,4,2,64,128]{4,3,2,1,0:T(8,128)S(1)}, u32[]{:S(2)}, u32[]{:S(2)}) collective-permute-start(f32[2,4,2,64,128]{4,3,2,1,0:T(8,128)S(1)} %dynamic-slice_bitcast_fusion.ready_ref), channel_id=1, source_target_pairs={{0,32},{32,0},{1,33},{33,1},{2,34},{34,2},{3,35},{35,3},{4,36},{36... | collective-permute-start | bytes 1572872 | tf_op jit(solution)/shard_map/ppermute | solution.py:46
  50.6 22.3 %all-to-all-start.1 = ((f32[16,32,128]{2,1,0:T(8,128)}), f32[16,32,128]{2,1,0:T(8,128)S(1)}, u32[]{:S(2)}, u32[]{:S(2)}) async-start(f32[16,32,128]{2,1,0:T(8,128)} %sum_copies.2), calls=%async_computation.1 | async-start | bytes 524288 | tf_op jit(solution)/shard_map/all_to_all | solution.py:22
  73.8 28.5 %copy-start = (f32[2048,128]{1,0:T(8,128)S(1)}, f32[2048,128]{1,0:T(8,128)}, u32[]{:S(2)}) copy-start(f32[2048,128]{1,0:T(8,128)} %weights_ref.3) | copy-start | bytes 3145732
  73.8 24.9 %all-to-all-start.2 = ((f32[32,32,128]{2,1,0:T(8,128)}), f32[32,32,128]{2,1,0:T(8,128)S(1)}, u32[]{:S(2)}, u32[]{:S(2)}) async-start(f32[32,32,128]{2,1,0:T(8,128)} %sum_copies.3), calls=%async_computation.2 | async-start | bytes 1048576 | tf_op jit(solution)/shard_map/all_to_all | solution.py:22
  82.2 15.7 %collective-permute-start.3 = (f32[2,4,64,128]{3,2,1,0:T(8,128)S(1)}, f32[2,4,64,128]{3,2,1,0:T(8,128)S(1)}, u32[]{:S(2)}, u32[]{:S(2)}) collective-permute-start(f32[2,4,64,128]{3,2,1,0:T(8,128)S(1)} %dynamic-slice_bitcast_fusion.1.ready_ref), channel_id=1, source_target_pairs={{0,64},{64,0},{1,65},{65,1},{2,66},{66,2},{3,67},{67,3},{4,68},{68... | collective-permute-start | bytes 786440 | tf_op jit(solution)/shard_map/ppermute | solution.py:46
  98.0 4.3 %copy-start.2 = (f32[2048]{0:T(1024)S(1)}, f32[2048]{0:T(1024)}, u32[]{:S(2)}) copy-start(f32[2048]{0:T(1024)} %param.17) | copy-start | bytes 24580
  98.7 5.1 %collective-permute-start.4 = (f32[1024,128]{1,0:T(8,128)S(1)}, f32[1024,128]{1,0:T(8,128)S(1)}, u32[]{:S(2)}, u32[]{:S(2)}) collective-permute-start(f32[1024,128]{1,0:T(8,128)S(1)} %bitcast.28), channel_id=1, source_target_pairs={{0,16},{16,0},{1,17},{17,1},{2,18},{18,2},{3,19},{19,3},{4,20},{20... | collective-permute-start | bytes 1572872 | tf_op jit(solution)/shard_map/ppermute | solution.py:46

commit v5 on v4

--- a/solution.py
+++ b/solution.py
@@ -50,69 +50,92 @@
     return lax.dynamic_index_in_dim(value, place, axis, keepdims=False)
 
 
-def sum_kernel(first_ref, ids_ref, rows_ref, *refs):
-    arrived, out_ref = refs[:-1], refs[-1]
-    width = rows_ref.shape[1]
-    value = rows_ref[...]
+def three_parts(value):
     high = value.astype(jnp.bfloat16)
     rest = value - high.astype(jnp.float32)
     middle = rest.astype(jnp.bfloat16)
     low = (rest - middle.astype(jnp.float32)).astype(jnp.bfloat16)
-    three = jnp.concatenate([high, middle, low], axis=1)
-    ids = ids_ref[...] - first_ref[0]
+    return jnp.concatenate([high, middle, low], axis=1)
+
+
+def tile_sum(ids, three, tile):
+    row = lax.broadcasted_iota(jnp.int32, (TILE, ids.shape[1]), 0) + tile * TILE
+    hit = jnp.where(row == ids, 1.0, 0.0).astype(jnp.bfloat16)
+    part = jnp.dot(hit, three, preferred_element_type=jnp.float32)
+    width = three.shape[1] // 3
+    return part[:, :width] + part[:, width : 2 * width] + part[:, 2 * width :]
+
+
+def sum_kernel(core_ref, ids_ref, rows_ref, arrived_ref, out_ref):
+    three = three_parts(rows_ref[...])
+    ids = ids_ref[...] - core_ref[0] * out_ref.shape[0]
     for tile in range(out_ref.shape[0] // TILE):
-        row = lax.broadcasted_iota(jnp.int32, (TILE, ids.shape[1]), 0) + tile * TILE
-        hit = jnp.where(row == ids, 1.0, 0.0).astype(jnp.bfloat16)
-        part = jnp.dot(hit, three, preferred_element_type=jnp.float32)
-        total = part[:, :width] + part[:, width : 2 * width] + part[:, 2 * width :]
         here = slice(tile * TILE, (tile + 1) * TILE)
-        out_ref[here, :] = total + arrived[0][here, :] if arrived else total
-
-
-def partial_grad(ids, rows_grad, first, rows, *arrived):
+        out_ref[here, :] = tile_sum(ids, three, tile) + arrived_ref[here, :]
+
+
+def own_half(core, ids, rows_grad, arrived):
     lookups, width = rows_grad.shape
+    rows = arrived.shape[0]
     whole = pl.BlockSpec(memory_space=pltpu.VMEM)
     return pl.pallas_call(
         sum_kernel,
         out_shape=jax.ShapeDtypeStruct((rows, width), jnp.float32),
-        in_specs=[pl.BlockSpec(memory_space=pltpu.SMEM), whole, whole] + [whole] * len(arrived),
+        in_specs=[pl.BlockSpec(memory_space=pltpu.SMEM), whole, whole, whole],
         out_specs=whole,
-        cost_estimate=pl.CostEstimate(flops=6 * rows * lookups * width, bytes_accessed=4 * (lookups + rows) * width, transcendentals=0),
-        compiler_params=pltpu.CompilerParams(vmem_limit_bytes=(24 if arrived else 56) << 20),
+        cost_estimate=pl.CostEstimate(flops=6 * rows * lookups * width, bytes_accessed=4 * (lookups + 2 * rows) * width, transcendentals=0),
+        compiler_params=pltpu.CompilerParams(vmem_limit_bytes=24 << 20),
         name="hot_rows_sum",
-    )(first.reshape(1), ids.reshape(1, lookups), rows_grad, *arrived)
-
-
-def coded_kernel(ids_ref, counts_ref, column_ref, core_ref, coef_ref, cold_ref, kept_ref, sent_ref):
-    slot, core, column = pl.program_id(0), core_ref[0], column_ref[0]
-    live = jnp.where(slot < counts_ref[0, 0], 1.0, 0.0)
-    kept, sent = cold_ref[0, :, core] * live, cold_ref[0, :, 1 - core] * live
-    for parity in range(kept_ref.shape[0]):
-        kept_ref[parity, 0] = coef_ref[parity, column] * kept
-        sent_ref[parity, 0] = coef_ref[parity, column] * sent
-
-
-def coded(cold_table, block_ids, counts, group_map, coef, core):
-    parities, slots = coef.shape[0], block_ids.shape[2]
+    )(core.reshape(1), ids, rows_grad, arrived)
+
+
+def front_kernel(core_ref, blocks_ref, counts_ref, column_ref, coef_ref, ids_ref, rows_ref, cold_ref, *refs):
+    outs, (blocks, *made, came, left) = refs[:3], refs[3:]
+    theirs, kept, sent = made
+    slots, half = blocks.shape[0], theirs.shape[0]
+    core, column = core_ref[0], column_ref[0]
+    loads = [pltpu.make_async_copy(cold_ref.at[blocks_ref[0, 0, s]], blocks.at[s], came.at[s]) for s in range(slots)]
+    for load in loads:
+        load.start()
+    three = three_parts(rows_ref[...])
+    ids = ids_ref[...] - (1 - core) * half
+    for tile in range(half // TILE):
+        theirs[tile * TILE : (tile + 1) * TILE, :] = tile_sum(ids, three, tile)
+    stores = [pltpu.make_async_copy(theirs, outs[0], left.at[0])]
+    stores[0].start()
+    for s in range(slots):
+        loads[s].wait()
+        live = jnp.where(s < counts_ref[0, 0], 1.0, 0.0)
+        for parity in range(kept.shape[0]):
+            scale = coef_ref[parity, column] * live
+            kept[parity, s] = scale * blocks[s, :, core]
+            sent[parity, s] = scale * blocks[s, :, 1 - core]
+        for place, (made_here, out) in enumerate(((kept, outs[1]), (sent, outs[2]))):
+            store = pltpu.make_async_copy(made_here.at[:, s], out.at[:, s], left.at[1 + 2 * s + place])
+            store.start()
+            stores.append(store)
+    for store in stores:
+        store.wait()
+
+
+def front(core, block_ids, counts, group_map, coef, ids, rows_grad, cold_table, half):
+    slots, parities, width = block_ids.shape[2], coef.shape[0], rows_grad.shape[1]
     rest = cold_table.shape[1:]
-    shape = (parities, slots, rest[0]) + rest[2:]
-    out = pl.BlockSpec((parities, 1) + shape[2:], lambda s, *refs: (0, s, 0, 0, 0))
-    return pl.pallas_call(
-        coded_kernel,
-        grid_spec=pltpu.PrefetchScalarGridSpec(
-            num_scalar_prefetch=4,
-            grid=(slots,),
-            in_specs=[
-                pl.BlockSpec(memory_space=pltpu.SMEM),
-                pl.BlockSpec((1,) + rest, lambda s, ids, *refs: (ids[0, 0, s], 0, 0, 0, 0)),
-            ],
-            out_specs=[out, out],
-        ),
-        out_shape=[jax.ShapeDtypeStruct(shape, jnp.float32)] * 2,
-        cost_estimate=pl.CostEstimate(flops=cold_table.size * 3, bytes_accessed=12 * cold_table.size, transcendentals=0),
-        compiler_params=pltpu.CompilerParams(vmem_limit_bytes=24 << 20),
-        name="coded_blocks",
-    )(block_ids, counts, group_map, core.reshape(1), coef, cold_table)
+    coded = jax.ShapeDtypeStruct((parities, slots, rest[0]) + rest[2:], jnp.float32)
+    outs = [jax.ShapeDtypeStruct((half, width), jnp.float32), coded, coded]
+    scalar, whole, apart = (pl.BlockSpec(memory_space=space) for space in (pltpu.SMEM, pltpu.VMEM, pl.ANY))
+    return pl.pallas_call(
+        front_kernel,
+        out_shape=outs,
+        in_specs=[scalar] * 5 + [whole] * 2 + [apart],
+        out_specs=[apart] * 3,
+        scratch_shapes=[pltpu.VMEM((slots,) + rest, jnp.float32)]
+        + [pltpu.VMEM(out.shape, out.dtype) for out in outs]
+        + [pltpu.SemaphoreType.DMA((slots,)), pltpu.SemaphoreType.DMA((1 + 2 * slots,))],
+        cost_estimate=pl.CostEstimate(flops=6 * half * rows_grad.size, bytes_accessed=4 << 20, transcendentals=0),
+        compiler_params=pltpu.CompilerParams(vmem_limit_bytes=56 << 20),
+        name="front",
+    )(core.reshape(1), block_ids, counts, group_map, coef, ids, rows_grad, cold_table)
 
 
 def adagrad_kernel(place_ref, grad_ref, weights_ref, accum_ref, *refs):
@@ -161,14 +184,11 @@
     core = lax.axis_index("core")
 
     half = hot_rows // 2
-    theirs = partial_grad(batch_ids[0, 0], out_grad[0, 0], (1 - core) * half, half)
+    ids, rows_grad = batch_ids[0], out_grad[0, 0]
+    table = cold_table[0, 0].reshape(-1, 4, 2, part_rows, width)
+    theirs, parity, away = front(core, block_ids, counts, group_map, coef, ids, rows_grad, table, half)
     arrived = swap(theirs, "core")
-
-    grad = partial_grad(batch_ids[0, 0], out_grad[0, 0], core * half, half, arrived)
-
-    cold_table, theirs = lax.optimization_barrier((cold_table, theirs))
-    table = cold_table[0, 0].reshape(-1, 4, 2, part_rows, width)
-    parity, away = coded(table, block_ids, counts, group_map, coef, core)
+    grad = own_half(core, ids, rows_grad, arrived)
     parity = parity + swap(away, "core")
     parity = parity.reshape(2, slot_count, 2, 2, part_rows, width)
     near_y, far_y = lax.axis_index("yl"), lax.axis_index("ym")

time: 106 us -> 104 us (0.981)
    pallas_call x3 -> x2, Pallas kernels: 6.79 us -> 6.07 us  [the longest x1 3.98 us: front(): pl.pallas_call(front_kernel, out_shape=outs, in_specs=[scalar] * 5 + [who...]
  transfers between devices with their start and end apart: 8 -> 8, of which waited for: 4 -> 4; matrix products, arithmetic and copies ran while one was open for 2% -> 2% of each run, Pallas kernels for 5% -> 4%
where the time goes in v5:
time: 104 us
  starting transfers between devices  52.5 us (50%)
  waiting for transfers between devices  35.7 us (34%)
  Pallas kernels  10.3 us (10%)
  other arithmetic  2.17 us (2%)
  between operations  2.12 us (2%)
  local copies, waits for them, and re-layouts  1.07 us (1%)
    ppermute x5, starting transfers between devices, swap(): return lax.ppermute(value, axis, [(0, 1), (1, 0)])  27.2 us
    all_to_all x3, starting transfers between devices, exchange(): return lax.all_to_all(parts, axes, 0, 0, tiled=True)  25.3 us
    all_to_all x3, waiting for transfers between devices, exchange(): return lax.all_to_all(parts, axes, 0, 0, tiled=True)  22.3 us
    ppermute x5, waiting for transfers between devices, swap(): return lax.ppermute(value, axis, [(0, 1), (1, 0)])  13.4 us
    pallas_call x1, Pallas kernels, front(): pl.pallas_call(front_kernel, out_shape=outs, in_specs=[scalar] * 5 + [who...  3.98 us
    pallas_call x2, Pallas kernels, adagrad_half(): pl.pallas_call(adagrad_kernel, grid_spec=pltpu.PrefetchScalarGridSpec(num...  2.62 us
    pallas_call x1, Pallas kernels, own_half(): pl.pallas_call(sum_kernel, out_shape=jax.ShapeDtypeStruct((rows, width),...  2.09 us
  transfers between devices with their start and end apart: 8, of which 4 were waited for; matrix products, arithmetic and copies ran while one was open for 2% of the time, Pallas kernels for 4%

profile of v5, /device:TPU:1, one launch (start us, length us, event | category | flops | bytes accessed | tf_op | source)
XLA Modules:
  0.0 103.8 jit_solution(14156057765441299692)
XLA Ops:
  1.9 0.0 copy-start.2
  1.9 0.0 copy-start.3
  1.9 4.0 %front.1 = (f32[1024,128]{1,0:T(8,128)}, f32[2,4,4,64,128]{4,3,2,1,0:T(8,128)}, f32[2,4,4,64,128]{4,3,2,1,0:T(8,128)}) custom-call(s32[1]{0:T(128)} %bitcast.core_ref.place_ref, s32[1,1,4]{2,1,0:T(1,128)} %blocks_ref.1, s32[1,1]{1,0:T(1,128)S(6)} %copy.20.counts_ref, s32[1]{0:T(128)S(6)} %copy.21.column_ref, f32[2,8]{1,0:T(2,128)} %coef_ref.1, ...), custom_call_target="tpu_custom_call" | custom-call | flops 805306368 | bytes 4194304 | tf_op jit(solution)/shard_map/front/pallas_call | solution.py:127
  5.9 16.1 %collective-permute-start = (f32[1024,128]{1,0:T(8,128)}, f32[1024,128]{1,0:T(8,128)S(1)}, u32[]{:S(2)}, u32[]{:S(2)}) collective-permute-start(f32[1024,128]{1,0:T(8,128)} %get-tuple-element.12), channel_id=1, source_target_pairs={{0,16},{16,0},{1,17},{17,1},{2,18},{18,2},{3,19},{19,3},{4,20},{20... | collective-permute-start | bytes 1572872 | tf_op jit(solution)/shard_map/ppermute | solution.py:46
  22.0 1.9 %collective-permute-start.1 = (f32[2,4,4,64,128]{4,3,2,1,0:T(8,128)}, f32[2,4,4,64,128]{4,3,2,1,0:T(8,128)S(1)}, u32[]{:S(2)}, u32[]{:S(2)}) collective-permute-start(f32[2,4,4,64,128]{4,3,2,1,0:T(8,128)} %get-tuple-element.14), channel_id=1, source_target_pairs={{0,16},{16,0},{1,17},{17,1},{2,18},{18,2},{3,19},{19,3},{4,20},{20... | collective-permute-start | bytes 3145736 | tf_op jit(solution)/shard_map/ppermute | solution.py:46
  23.9 0.0 collective-permute-done.arrived_ref
  23.9 0.0 copy-done.2
  23.9 0.0 copy-done.3
  24.0 2.1 %hot_rows_sum.1 = f32[1024,128]{1,0:T(8,128)} custom-call(s32[1]{0:T(128)} %bitcast.core_ref.place_ref, s32[1,1024]{1,0:T(1,128)S(1)} %bitcast.33, f32[1024,128]{1,0:T(8,128)S(1)} %bitcast.31, f32[1024,128]{1,0:T(8,128)S(1)} %collective-permute-done.arrived_ref), custom_call_target="tpu_custom_call" | custom-call | flops 805306368 | bytes 1572864 | tf_op jit(solution)/shard_map/hot_rows_sum/pallas_call | solution.py:81
  26.0 6.3 %all-to-all-start = ((f32[32,32,128]{2,1,0:T(8,128)}), f32[32,32,128]{2,1,0:T(8,128)S(1)}, u32[]{:S(2)}, u32[]{:S(2)}) async-start(f32[32,32,128]{2,1,0:T(8,128)} %bitcast.4), calls=%async_computation | async-start | bytes 1048576 | tf_op jit(solution)/shard_map/all_to_all | solution.py:22
  32.4 0.0 collective-permute-done.1
  32.4 0.0 copy-start.5
  32.4 1.0 copy-done.5
  33.4 1.4 %add.25 = f32[2,4,4,64,128]{4,3,2,1,0:T(8,128)S(1)} add(f32[2,4,4,64,128]{4,3,2,1,0:T(8,128)S(1)} %copy-done.4, f32[2,4,4,64,128]{4,3,2,1,0:T(8,128)} %copy-done.5) | non-fusion elementwise | flops 262144 | bytes 3145728 | tf_op jit(solution)/shard_map/add | solution.py:192
  34.7 0.1 dynamic-slice_bitcast_fusion.ready_ref
  34.8 3.1 %collective-permute-start.2 = (f32[2,4,2,64,128]{4,3,2,1,0:T(8,128)S(1)}, f32[2,4,2,64,128]{4,3,2,1,0:T(8,128)S(1)}, u32[]{:S(2)}, u32[]{:S(2)}) collective-permute-start(f32[2,4,2,64,128]{4,3,2,1,0:T(8,128)S(1)} %dynamic-slice_bitcast_fusion.ready_ref), channel_id=1, source_target_pairs={{0,32},{32,0},{1,33},{33,1},{2,34},{34,2},{3,35},{35,3},{4,36},{36... | collective-permute-start | bytes 1572872 | tf_op jit(solution)/shard_map/ppermute | solution.py:46
  38.0 10.6 %all-to-all-done.parts_ref = f32[32,32,128]{2,1,0:T(8,128)S(1)} async-done(((f32[32,32,128]{2,1,0:T(8,128)}), f32[32,32,128]{2,1,0:T(8,128)S(1)}, u32[]{:S(2)}, u32[]{:S(2)}) %all-to-all-start) | async-done | bytes 524320 | tf_op jit(solution)/shard_map/all_to_all | solution.py:22
  48.6 0.8 sum_copies.2
  49.3 10.5 %all-to-all-start.1 = ((f32[16,32,128]{2,1,0:T(8,128)}), f32[16,32,128]{2,1,0:T(8,128)S(1)}, u32[]{:S(2)}, u32[]{:S(2)}) async-start(f32[16,32,128]{2,1,0:T(8,128)} %sum_copies.2), calls=%async_computation.1 | async-start | bytes 524288 | tf_op jit(solution)/shard_map/all_to_all | solution.py:22
  59.9 0.0 collective-permute-done.2
  59.9 0.1 bitcast_add_fusion
  60.0 11.7 %all-to-all-done.1.parts_ref = f32[16,32,128]{2,1,0:T(8,128)S(1)} async-done(((f32[16,32,128]{2,1,0:T(8,128)}), f32[16,32,128]{2,1,0:T(8,128)S(1)}, u32[]{:S(2)}, u32[]{:S(2)}) %all-to-all-start.1) | async-done | bytes 262176 | tf_op jit(solution)/shard_map/all_to_all | solution.py:22
  71.7 0.9 sum_copies.3
  72.5 8.4 %all-to-all-start.2 = ((f32[32,32,128]{2,1,0:T(8,128)}), f32[32,32,128]{2,1,0:T(8,128)S(1)}, u32[]{:S(2)}, u32[]{:S(2)}) async-start(f32[32,32,128]{2,1,0:T(8,128)} %sum_copies.3), calls=%async_computation.2 | async-start | bytes 1048576 | tf_op jit(solution)/shard_map/all_to_all | solution.py:22
  80.9 2.5 %collective-permute-start.3 = (f32[2,4,64,128]{3,2,1,0:T(8,128)S(1)}, f32[2,4,64,128]{3,2,1,0:T(8,128)S(1)}, u32[]{:S(2)}, u32[]{:S(2)}) collective-permute-start(f32[2,4,64,128]{3,2,1,0:T(8,128)S(1)} %dynamic-slice_bitcast_fusion.1.ready_ref), channel_id=1, source_target_pairs={{0,64},{64,0},{1,65},{65,1},{2,66},{66,2},{3,67},{67,3},{4,68},{68... | collective-permute-start | bytes 786440 | tf_op jit(solution)/shard_map/ppermute | solution.py:46
  83.4 13.2 %collective-permute-done.3 = f32[2,4,64,128]{3,2,1,0:T(8,128)S(1)} collective-permute-done((f32[2,4,64,128]{3,2,1,0:T(8,128)S(1)}, f32[2,4,64,128]{3,2,1,0:T(8,128)S(1)}, u32[]{:S(2)}, u32[]{:S(2)}) %collective-permute-start.3) | collective-permute-done | bytes 262176 | tf_op jit(solution)/shard_map/ppermute | solution.py:46
  96.7 0.7 fusion
  97.4 0.0 all-to-all-done.2
  97.4 3.6 %collective-permute-start.4 = (f32[1024,128]{1,0:T(8,128)S(1)}, f32[1024,128]{1,0:T(8,128)S(1)}, u32[]{:S(2)}, u32[]{:S(2)}) collective-permute-start(f32[1024,128]{1,0:T(8,128)S(1)} %bitcast.26), channel_id=1, source_target_pairs={{0,16},{16,0},{1,17},{17,1},{2,18},{18,2},{3,19},{19,3},{4,20},{20... | collective-permute-start | bytes 1572872 | tf_op jit(solution)/shard_map/ppermute | solution.py:46
  101.0 1.3 %hot_rows_adagrad.2 = (f32[2048,128]{1,0:T(8,128)}, f32[16,128]{1,0:T(8,128)}) custom-call(s32[1]{0:T(128)} %bitcast.core_ref.place_ref, f32[1024,128]{1,0:T(8,128)S(1)} %bitcast.27, f32[2048,128]{1,0:T(8,128)S(1)} %copy-done, f32[16,128]{1,0:T(8,128)S(1)} %bitcast.28), custom_call_target="tpu_custom_call" | custom-call | flops 1048576 | bytes 1572864 | tf_op jit(solution)/shard_map/hot_rows_adagrad/pallas_call | solution.py:157
  102.3 0.2 collective-permute-done.4.grad_ref
  102.5 1.3 %hot_rows_adagrad.3 = (f32[2048,128]{1,0:T(8,128)}, f32[16,128]{1,0:T(8,128)}) custom-call(s32[1]{0:T(128)} %bitcast.12.place_ref, f32[1024,128]{1,0:T(8,128)S(1)} %collective-permute-done.4.grad_ref, f32[2048,128]{1,0:T(8,128)S(1)} %copy-done, f32[16,128]{1,0:T(8,128)S(1)} %bitcast.29, ...), custom_call_target="tpu_custom_call", output_to_operand_aliasing={{0}: (4, {}), {1}: (5, {})} | custom-call | flops 1048576 | bytes 1572864 | tf_op jit(solution)/shard_map/hot_rows_adagrad/pallas_call | solution.py:157
  (7 shorter events, 0.0 us)
Async XLA Ops:
  1.9 22.0 %copy-start.2 = (f32[1,1,1024,128]{3,2,1,0:T(8,128)S(1)}, f32[1,1,1024,128]{3,2,1,0:T(8,128)}, u32[]{:S(2)}) copy-start(f32[1,1,1024,128]{3,2,1,0:T(8,128)} %param.15) | copy-start | bytes 1572868
  1.9 22.0 %copy-start.3 = (s32[1,1,1024]{2,1,0:T(1,128)S(1)}, s32[1,1,1024]{2,1,0:T(1,128)}, u32[]{:S(2)}) copy-start(s32[1,1,1024]{2,1,0:T(1,128)} %param.14) | copy-start | bytes 12292
  5.9 18.0 %collective-permute-start = (f32[1024,128]{1,0:T(8,128)}, f32[1024,128]{1,0:T(8,128)S(1)}, u32[]{:S(2)}, u32[]{:S(2)}) collective-permute-start(f32[1024,128]{1,0:T(8,128)} %get-tuple-element.12), channel_id=1, source_target_pairs={{0,16},{16,0},{1,17},{17,1},{2,18},{18,2},{3,19},{19,3},{4,20},{20... | collective-permute-start | bytes 1572872 | tf_op jit(solution)/shard_map/ppermute | solution.py:46
  22.0 10.4 %collective-permute-start.1 = (f32[2,4,4,64,128]{4,3,2,1,0:T(8,128)}, f32[2,4,4,64,128]{4,3,2,1,0:T(8,128)S(1)}, u32[]{:S(2)}, u32[]{:S(2)}) collective-permute-start(f32[2,4,4,64,128]{4,3,2,1,0:T(8,128)} %get-tuple-element.14), channel_id=1, source_target_pairs={{0,16},{16,0},{1,17},{17,1},{2,18},{18,2},{3,19},{19,3},{4,20},{20... | collective-permute-start | bytes 3145736 | tf_op jit(solution)/shard_map/ppermute | solution.py:46
  26.0 7.3 %copy-start.4 = (f32[2,4,4,64,128]{4,3,2,1,0:T(8,128)S(1)}, f32[2,4,4,64,128]{4,3,2,1,0:T(8,128)}, u32[]{:S(2)}) copy-start(f32[2,4,4,64,128]{4,3,2,1,0:T(8,128)} %get-tuple-element.13) | copy-start | bytes 3145732
  26.0 22.5 %all-to-all-start = ((f32[32,32,128]{2,1,0:T(8,128)}), f32[32,32,128]{2,1,0:T(8,128)S(1)}, u32[]{:S(2)}, u32[]{:S(2)}) async-start(f32[32,32,128]{2,1,0:T(8,128)} %bitcast.4), calls=%async_computation | async-start | bytes 1048576 | tf_op jit(solution)/shard_map/all_to_all | solution.py:22
  32.4 1.0 copy-start.5
  34.8 25.1 %collective-permute-start.2 = (f32[2,4,2,64,128]{4,3,2,1,0:T(8,128)S(1)}, f32[2,4,2,64,128]{4,3,2,1,0:T(8,128)S(1)}, u32[]{:S(2)}, u32[]{:S(2)}) collective-permute-start(f32[2,4,2,64,128]{4,3,2,1,0:T(8,128)S(1)} %dynamic-slice_bitcast_fusion.ready_ref), channel_id=1, source_target_pairs={{0,32},{32,0},{1,33},{33,1},{2,34},{34,2},{3,35},{35,3},{4,36},{36... | collective-permute-start | bytes 1572872 | tf_op jit(solution)/shard_map/ppermute | solution.py:46
  49.3 22.3 %all-to-all-start.1 = ((f32[16,32,128]{2,1,0:T(8,128)}), f32[16,32,128]{2,1,0:T(8,128)S(1)}, u32[]{:S(2)}, u32[]{:S(2)}) async-start(f32[16,32,128]{2,1,0:T(8,128)} %sum_copies.2), calls=%async_computation.1 | async-start | bytes 524288 | tf_op jit(solution)/shard_map/all_to_all | solution.py:22
  72.5 28.5 %copy-start = (f32[2048,128]{1,0:T(8,128)S(1)}, f32[2048,128]{1,0:T(8,128)}, u32[]{:S(2)}) copy-start(f32[2048,128]{1,0:T(8,128)} %weights_ref.3) | copy-start | bytes 3145732
  72.5 24.9 %all-to-all-start.2 = ((f32[32,32,128]{2,1,0:T(8,128)}), f32[32,32,128]{2,1,0:T(8,128)S(1)}, u32[]{:S(2)}, u32[]{:S(2)}) async-start(f32[32,32,128]{2,1,0:T(8,128)} %sum_copies.3), calls=%async_computation.2 | async-start | bytes 1048576 | tf_op jit(solution)/shard_map/all_to_all | solution.py:22
  80.9 15.7 %collective-permute-start.3 = (f32[2,4,64,128]{3,2,1,0:T(8,128)S(1)}, f32[2,4,64,128]{3,2,1,0:T(8,128)S(1)}, u32[]{:S(2)}, u32[]{:S(2)}) collective-permute-start(f32[2,4,64,128]{3,2,1,0:T(8,128)S(1)} %dynamic-slice_bitcast_fusion.1.ready_ref), channel_id=1, source_target_pairs={{0,64},{64,0},{1,65},{65,1},{2,66},{66,2},{3,67},{67,3},{4,68},{68... | collective-permute-start | bytes 786440 | tf_op jit(solution)/shard_map/ppermute | solution.py:46
  96.7 4.3 %copy-start.1 = (f32[2048]{0:T(1024)S(1)}, f32[2048]{0:T(1024)}, u32[]{:S(2)}) copy-start(f32[2048]{0:T(1024)} %param.17) | copy-start | bytes 24580
  97.4 5.1 %collective-permute-start.4 = (f32[1024,128]{1,0:T(8,128)S(1)}, f32[1024,128]{1,0:T(8,128)S(1)}, u32[]{:S(2)}, u32[]{:S(2)}) collective-permute-start(f32[1024,128]{1,0:T(8,128)S(1)} %bitcast.26), channel_id=1, source_target_pairs={{0,16},{16,0},{1,17},{17,1},{2,18},{18,2},{3,19},{19,3},{4,20},{20... | collective-permute-start | bytes 1572872 | tf_op jit(solution)/shard_map/ppermute | solution.py:46

commit v6 on v5

--- a/solution.py
+++ b/solution.py
@@ -9,9 +9,9 @@
 SIZES = (2, 2, 2, 2, 2, 2, 2, 8)
 CODE = ("xh", "xm", "yh", "ym", "yl", "core")
 DP = ("xl", "z")
-NEAR = ("yl", "xl", "z")
+NEAR = ("xh", "xm", "xl", "z")
 TILE = 256
-FAR = ("xh", "xm", "yh", "ym")
+FAR = ("yh", "ym", "yl")
 
 
 def size(axes):
@@ -66,27 +66,41 @@
     return part[:, :width] + part[:, width : 2 * width] + part[:, 2 * width :]
 
 
-def sum_kernel(core_ref, ids_ref, rows_ref, arrived_ref, out_ref):
+def sum_kernel(core_ref, ids_ref, rows_ref, out_ref):
     three = three_parts(rows_ref[...])
     ids = ids_ref[...] - core_ref[0] * out_ref.shape[0]
     for tile in range(out_ref.shape[0] // TILE):
         here = slice(tile * TILE, (tile + 1) * TILE)
-        out_ref[here, :] = tile_sum(ids, three, tile) + arrived_ref[here, :]
-
-
-def own_half(core, ids, rows_grad, arrived):
+        out_ref[here, :] = tile_sum(ids, three, tile)
+
+
+def add_kernel(left_ref, right_ref, out_ref):
+    out_ref[...] = left_ref[...] + right_ref[...]
+
+
+def added(left, right):
+    return pl.pallas_call(
+        add_kernel,
+        out_shape=jax.ShapeDtypeStruct(left.shape, left.dtype),
+        in_specs=[pl.BlockSpec(memory_space=pltpu.VMEM)] * 2,
+        out_specs=pl.BlockSpec(memory_space=pltpu.VMEM),
+        compiler_params=pltpu.CompilerParams(vmem_limit_bytes=24 << 20),
+        name="added",
+    )(left, right)
+
+
+def own_half(core, ids, rows_grad, rows):
     lookups, width = rows_grad.shape
-    rows = arrived.shape[0]
     whole = pl.BlockSpec(memory_space=pltpu.VMEM)
     return pl.pallas_call(
         sum_kernel,
         out_shape=jax.ShapeDtypeStruct((rows, width), jnp.float32),
-        in_specs=[pl.BlockSpec(memory_space=pltpu.SMEM), whole, whole, whole],
+        in_specs=[pl.BlockSpec(memory_space=pltpu.SMEM), whole, whole],
         out_specs=whole,
-        cost_estimate=pl.CostEstimate(flops=6 * rows * lookups * width, bytes_accessed=4 * (lookups + 2 * rows) * width, transcendentals=0),
+        cost_estimate=pl.CostEstimate(flops=6 * rows * lookups * width, bytes_accessed=4 * (lookups + rows) * width, transcendentals=0),
         compiler_params=pltpu.CompilerParams(vmem_limit_bytes=24 << 20),
         name="hot_rows_sum",
-    )(core.reshape(1), ids, rows_grad, arrived)
+    )(core.reshape(1), ids, rows_grad)
 
 
 def front_kernel(core_ref, blocks_ref, counts_ref, column_ref, coef_ref, ids_ref, rows_ref, cold_ref, *refs):
@@ -188,20 +202,22 @@
     table = cold_table[0, 0].reshape(-1, 4, 2, part_rows, width)
     theirs, parity, away = front(core, block_ids, counts, group_map, coef, ids, rows_grad, table, half)
     arrived = swap(theirs, "core")
-    grad = own_half(core, ids, rows_grad, arrived)
+    grad = added(own_half(core, ids, rows_grad, half), arrived)
+    away, grad = lax.optimization_barrier((away, grad))
     parity = parity + swap(away, "core")
     parity = parity.reshape(2, slot_count, 2, 2, part_rows, width)
     near_y, far_y = lax.axis_index("yl"), lax.axis_index("ym")
     send_near = pick(parity, 1 - near_y, 3)
     parity = pick(parity, near_y, 3) + swap(send_near, "yl")
     send_far = pick(parity, 1 - far_y, 2)
-    parity_shards = (pick(parity, far_y, 2) + swap(send_far, "ym"))[None, None]
+    mine, last = pick(parity, far_y, 2), swap(send_far, "ym")
 
     near = size(NEAR)
     parts = exchange(grad.reshape(near, half // near, width), NEAR)
     parts = exchange(sum_copies(parts, size(FAR), send_near), FAR)
     grad = exchange(sum_copies(parts, near, send_far), NEAR).reshape(half, width)
-    grad, parity_shards = lax.optimization_barrier((grad, parity_shards))
+    grad, last = lax.optimization_barrier((grad, last))
+    parity_shards = (mine + last)[None, None]
     other = swap(grad, "core")
     sums = accum.reshape(hot_rows // width, width)
     done = adagrad_half(core, grad, hot_weights, sums)

time: 104 us -> 104 us (level)
  waiting for transfers between devices: 35.7 us -> 33.3 us
  starting transfers between devices: 52.5 us -> 54 us
    all_to_all x3, waiting for transfers between devices: 22.3 us -> 18.7 us  [exchange(): return lax.all_to_all(parts, axes, 0, 0, tiled=True)]
    ppermute x5, starting transfers between devices: 27.2 us -> 29.9 us  [swap(): return lax.ppermute(value, axis, [(0, 1), (1, 0)])]
    all_to_all x3, starting transfers between devices: 25.3 us -> 24.1 us  [exchange(): return lax.all_to_all(parts, axes, 0, 0, tiled=True)]
    ppermute x5, waiting for transfers between devices: 13.4 us -> 14.5 us  [swap(): return lax.ppermute(value, axis, [(0, 1), (1, 0)])]
  transfers between devices with their start and end apart: 8 -> 8, of which waited for: 4 -> 4; matrix products, arithmetic and copies ran while one was open for 2% -> 2% of each run, Pallas kernels for 4% -> 3%
where the time goes in v6:
time: 104 us; the launch traced here: 103 us
  starting transfers between devices  54 us (52%)
  waiting for transfers between devices  33.3 us (32%)
  Pallas kernels  10.3 us (10%)
  other arithmetic  2.17 us (2%)
  between operations  2.13 us (2%)
  local copies, waits for them, and re-layouts  1.08 us (1%)
    ppermute x5, starting transfers between devices, swap(): return lax.ppermute(value, axis, [(0, 1), (1, 0)])  29.9 us
    all_to_all x3, starting transfers between devices, exchange(): return lax.all_to_all(parts, axes, 0, 0, tiled=True)  24.1 us
    all_to_all x3, waiting for transfers between devices, exchange(): return lax.all_to_all(parts, axes, 0, 0, tiled=True)  18.7 us
    ppermute x5, waiting for transfers between devices, swap(): return lax.ppermute(value, axis, [(0, 1), (1, 0)])  14.5 us
    pallas_call x1, Pallas kernels, front(): pl.pallas_call(front_kernel, out_shape=outs, in_specs=[scalar] * 5 + [who...  3.98 us
    pallas_call x2, Pallas kernels, adagrad_half(): pl.pallas_call(adagrad_kernel, grid_spec=pltpu.PrefetchScalarGridSpec(num...  2.62 us
  transfers between devices with their start and end apart: 8, of which 4 were waited for; matrix products, arithmetic and copies ran while one was open for 2% of the time, Pallas kernels for 3%

profile of v6, /device:TPU:1, one launch (start us, length us, event | category | flops | bytes accessed | tf_op | source)
XLA Modules:
  0.0 102.9 jit_solution(8863312378726727112)
XLA Ops:
  1.9 4.0 %front.1 = (f32[1024,128]{1,0:T(8,128)}, f32[2,4,4,64,128]{4,3,2,1,0:T(8,128)}, f32[2,4,4,64,128]{4,3,2,1,0:T(8,128)}) custom-call(s32[1]{0:T(128)} %bitcast.core_ref.place_ref, s32[1,1,4]{2,1,0:T(1,128)} %blocks_ref.1, s32[1,1]{1,0:T(1,128)S(6)} %copy.20.counts_ref, s32[1]{0:T(128)S(6)} %copy.21.column_ref, f32[2,8]{1,0:T(2,128)} %coef_ref.1, ...), custom_call_target="tpu_custom_call" | custom-call | flops 805306368 | bytes 4194304 | tf_op jit(solution)/shard_map/front/pallas_call | solution.py:141
  5.9 16.1 %collective-permute-start = (f32[1024,128]{1,0:T(8,128)}, f32[1024,128]{1,0:T(8,128)S(1)}, u32[]{:S(2)}, u32[]{:S(2)}) collective-permute-start(f32[1024,128]{1,0:T(8,128)} %get-tuple-element.16), channel_id=1, source_target_pairs={{0,16},{16,0},{1,17},{17,1},{2,18},{18,2},{3,19},{19,3},{4,20},{20... | collective-permute-start | bytes 1572872 | tf_op jit(solution)/shard_map/ppermute | solution.py:46
  22.0 1.3 %hot_rows_sum.1.left_ref = f32[1024,128]{1,0:T(8,128)S(1)} custom-call(s32[1]{0:T(128)} %bitcast.core_ref.place_ref, s32[1,1024]{1,0:T(1,128)S(1)} %bitcast.33, f32[1024,128]{1,0:T(8,128)S(1)} %bitcast.31), custom_call_target="tpu_custom_call" | custom-call | flops 805306368 | bytes 1048576 | tf_op jit(solution)/shard_map/hot_rows_sum/pallas_call | solution.py:95
  23.3 0.0 copy-start.4
  23.3 0.4 collective-permute-done.right_ref
  23.7 0.9 added.1
  24.6 2.3 %collective-permute-start.1 = (f32[2,4,4,64,128]{4,3,2,1,0:T(8,128)}, f32[2,4,4,64,128]{4,3,2,1,0:T(8,128)S(1)}, u32[]{:S(2)}, u32[]{:S(2)}) collective-permute-start(f32[2,4,4,64,128]{4,3,2,1,0:T(8,128)} %get-tuple-element.17), channel_id=1, source_target_pairs={{0,16},{16,0},{1,17},{17,1},{2,18},{18,2},{3,19},{19,3},{4,20},{20... | collective-permute-start | bytes 3145736 | tf_op jit(solution)/shard_map/ppermute | solution.py:46
  26.9 9.7 %all-to-all-start = ((f32[64,16,128]{2,1,0:T(8,128)}), f32[64,16,128]{2,1,0:T(8,128)S(1)}, u32[]{:S(2)}, u32[]{:S(2)}) async-start(f32[64,16,128]{2,1,0:T(8,128)} %bitcast.8), calls=%async_computation | async-start | bytes 1048576 | tf_op jit(solution)/shard_map/all_to_all | solution.py:22
  36.6 0.0 collective-permute-done.1
  36.6 1.0 copy-done.5
  37.6 0.0 copy-done.4
  37.6 1.4 %add.25 = f32[2,4,4,64,128]{4,3,2,1,0:T(8,128)S(1)} add(f32[2,4,4,64,128]{4,3,2,1,0:T(8,128)S(1)} %copy-done.4, f32[2,4,4,64,128]{4,3,2,1,0:T(8,128)} %copy-done.5) | non-fusion elementwise | flops 262144 | bytes 3145728 | tf_op jit(solution)/shard_map/add | solution.py:207
  38.9 0.1 dynamic-slice_bitcast_fusion.ready_ref
  39.0 3.3 %collective-permute-start.2 = (f32[2,4,2,64,128]{4,3,2,1,0:T(8,128)S(1)}, f32[2,4,2,64,128]{4,3,2,1,0:T(8,128)S(1)}, u32[]{:S(2)}, u32[]{:S(2)}) collective-permute-start(f32[2,4,2,64,128]{4,3,2,1,0:T(8,128)S(1)} %dynamic-slice_bitcast_fusion.ready_ref), channel_id=1, source_target_pairs={{0,32},{32,0},{1,33},{33,1},{2,34},{34,2},{3,35},{35,3},{4,36},{36... | collective-permute-start | bytes 1572872 | tf_op jit(solution)/shard_map/ppermute | solution.py:46
  42.3 11.5 %all-to-all-done.parts_ref = f32[64,16,128]{2,1,0:T(8,128)S(1)} async-done(((f32[64,16,128]{2,1,0:T(8,128)}), f32[64,16,128]{2,1,0:T(8,128)S(1)}, u32[]{:S(2)}, u32[]{:S(2)}) %all-to-all-start) | async-done | bytes 524320 | tf_op jit(solution)/shard_map/all_to_all | solution.py:22
  53.9 0.7 sum_copies.2
  54.6 7.3 %all-to-all-start.1 = ((f32[8,16,128]{2,1,0:T(8,128)}), f32[8,16,128]{2,1,0:T(8,128)S(1)}, u32[]{:S(2)}, u32[]{:S(2)}) async-start(f32[8,16,128]{2,1,0:T(8,128)} %sum_copies.2), calls=%async_computation.1 | async-start | bytes 131072 | tf_op jit(solution)/shard_map/all_to_all | solution.py:22
  61.9 0.0 collective-permute-done.2
  61.9 0.1 bitcast_add_fusion
  62.0 0.0 copy-start
  62.0 7.2 %all-to-all-done.1.parts_ref = f32[8,16,128]{2,1,0:T(8,128)S(1)} async-done(((f32[8,16,128]{2,1,0:T(8,128)}), f32[8,16,128]{2,1,0:T(8,128)S(1)}, u32[]{:S(2)}, u32[]{:S(2)}) %all-to-all-start.1) | async-done | bytes 65568 | tf_op jit(solution)/shard_map/all_to_all | solution.py:22
  69.2 0.8 sum_copies.3
  70.0 7.2 %all-to-all-start.2 = ((f32[64,16,128]{2,1,0:T(8,128)}), f32[64,16,128]{2,1,0:T(8,128)S(1)}, u32[]{:S(2)}, u32[]{:S(2)}) async-start(f32[64,16,128]{2,1,0:T(8,128)} %sum_copies.3), calls=%async_computation.2 | async-start | bytes 1048576 | tf_op jit(solution)/shard_map/all_to_all | solution.py:22
  77.2 0.0 copy-start.1
  77.2 2.3 %collective-permute-start.3 = (f32[2,4,64,128]{3,2,1,0:T(8,128)S(1)}, f32[2,4,64,128]{3,2,1,0:T(8,128)S(1)}, u32[]{:S(2)}, u32[]{:S(2)}) collective-permute-start(f32[2,4,64,128]{3,2,1,0:T(8,128)S(1)} %dynamic-slice_bitcast_fusion.1.ready_ref), channel_id=1, source_target_pairs={{0,64},{64,0},{1,65},{65,1},{2,66},{66,2},{3,67},{67,3},{4,68},{68... | collective-permute-start | bytes 786440 | tf_op jit(solution)/shard_map/ppermute | solution.py:46
  79.5 14.1 %collective-permute-done.3 = f32[2,4,64,128]{3,2,1,0:T(8,128)S(1)} collective-permute-done((f32[2,4,64,128]{3,2,1,0:T(8,128)S(1)}, f32[2,4,64,128]{3,2,1,0:T(8,128)S(1)}, u32[]{:S(2)}, u32[]{:S(2)}) %collective-permute-start.3) | collective-permute-done | bytes 262176 | tf_op jit(solution)/shard_map/ppermute | solution.py:46
  93.6 0.0 all-to-all-done.2
  93.6 6.0 %collective-permute-start.4 = (f32[1024,128]{1,0:T(8,128)S(1)}, f32[1024,128]{1,0:T(8,128)S(1)}, u32[]{:S(2)}, u32[]{:S(2)}) collective-permute-start(f32[1024,128]{1,0:T(8,128)S(1)} %bitcast.26), channel_id=1, source_target_pairs={{0,16},{16,0},{1,17},{17,1},{2,18},{18,2},{3,19},{19,3},{4,20},{20... | collective-permute-start | bytes 1572872 | tf_op jit(solution)/shard_map/ppermute | solution.py:46
  99.6 1.3 %hot_rows_adagrad.2 = (f32[2048,128]{1,0:T(8,128)}, f32[16,128]{1,0:T(8,128)}) custom-call(s32[1]{0:T(128)} %bitcast.core_ref.place_ref, f32[1024,128]{1,0:T(8,128)S(1)} %bitcast.27, f32[2048,128]{1,0:T(8,128)S(1)} %copy-done, f32[16,128]{1,0:T(8,128)S(1)} %bitcast.28), custom_call_target="tpu_custom_call" | custom-call | flops 1048576 | bytes 1572864 | tf_op jit(solution)/shard_map/hot_rows_adagrad/pallas_call | solution.py:171
  100.9 0.7 fusion
  101.6 0.0 collective-permute-done.4.grad_ref
  101.6 1.3 %hot_rows_adagrad.3 = (f32[2048,128]{1,0:T(8,128)}, f32[16,128]{1,0:T(8,128)}) custom-call(s32[1]{0:T(128)} %bitcast.12.place_ref, f32[1024,128]{1,0:T(8,128)S(1)} %collective-permute-done.4.grad_ref, f32[2048,128]{1,0:T(8,128)S(1)} %copy-done, f32[16,128]{1,0:T(8,128)S(1)} %bitcast.29, ...), custom_call_target="tpu_custom_call", output_to_operand_aliasing={{0}: (4, {}), {1}: (5, {})} | custom-call | flops 1048576 | bytes 1572864 | tf_op jit(solution)/shard_map/hot_rows_adagrad/pallas_call | solution.py:171
  (8 shorter events, 0.0 us)
Async XLA Ops:
  1.9 20.1 %copy-start.2 = (f32[1,1,1024,128]{3,2,1,0:T(8,128)S(1)}, f32[1,1,1024,128]{3,2,1,0:T(8,128)}, u32[]{:S(2)}) copy-start(f32[1,1,1024,128]{3,2,1,0:T(8,128)} %param.15) | copy-start | bytes 1572868
  1.9 20.1 %copy-start.3 = (s32[1,1,1024]{2,1,0:T(1,128)S(1)}, s32[1,1,1024]{2,1,0:T(1,128)}, u32[]{:S(2)}) copy-start(s32[1,1,1024]{2,1,0:T(1,128)} %param.14) | copy-start | bytes 12292
  5.9 17.8 %collective-permute-start = (f32[1024,128]{1,0:T(8,128)}, f32[1024,128]{1,0:T(8,128)S(1)}, u32[]{:S(2)}, u32[]{:S(2)}) collective-permute-start(f32[1024,128]{1,0:T(8,128)} %get-tuple-element.16), channel_id=1, source_target_pairs={{0,16},{16,0},{1,17},{17,1},{2,18},{18,2},{3,19},{19,3},{4,20},{20... | collective-permute-start | bytes 1572872 | tf_op jit(solution)/shard_map/ppermute | solution.py:46
  23.3 14.3 %copy-start.4 = (f32[2,4,4,64,128]{4,3,2,1,0:T(8,128)S(1)}, f32[2,4,4,64,128]{4,3,2,1,0:T(8,128)}, u32[]{:S(2)}) copy-start(f32[2,4,4,64,128]{4,3,2,1,0:T(8,128)} %get-tuple-element.14) | copy-start | bytes 3145732
  24.6 12.0 %collective-permute-start.1 = (f32[2,4,4,64,128]{4,3,2,1,0:T(8,128)}, f32[2,4,4,64,128]{4,3,2,1,0:T(8,128)S(1)}, u32[]{:S(2)}, u32[]{:S(2)}) collective-permute-start(f32[2,4,4,64,128]{4,3,2,1,0:T(8,128)} %get-tuple-element.17), channel_id=1, source_target_pairs={{0,16},{16,0},{1,17},{17,1},{2,18},{18,2},{3,19},{19,3},{4,20},{20... | collective-permute-start | bytes 3145736 | tf_op jit(solution)/shard_map/ppermute | solution.py:46
  26.9 27.0 %all-to-all-start = ((f32[64,16,128]{2,1,0:T(8,128)}), f32[64,16,128]{2,1,0:T(8,128)S(1)}, u32[]{:S(2)}, u32[]{:S(2)}) async-start(f32[64,16,128]{2,1,0:T(8,128)} %bitcast.8), calls=%async_computation | async-start | bytes 1048576 | tf_op jit(solution)/shard_map/all_to_all | solution.py:22
  36.6 1.0 copy-start.5
  39.0 22.9 %collective-permute-start.2 = (f32[2,4,2,64,128]{4,3,2,1,0:T(8,128)S(1)}, f32[2,4,2,64,128]{4,3,2,1,0:T(8,128)S(1)}, u32[]{:S(2)}, u32[]{:S(2)}) collective-permute-start(f32[2,4,2,64,128]{4,3,2,1,0:T(8,128)S(1)} %dynamic-slice_bitcast_fusion.ready_ref), channel_id=1, source_target_pairs={{0,32},{32,0},{1,33},{33,1},{2,34},{34,2},{3,35},{35,3},{4,36},{36... | collective-permute-start | bytes 1572872 | tf_op jit(solution)/shard_map/ppermute | solution.py:46
  54.6 14.6 %all-to-all-start.1 = ((f32[8,16,128]{2,1,0:T(8,128)}), f32[8,16,128]{2,1,0:T(8,128)S(1)}, u32[]{:S(2)}, u32[]{:S(2)}) async-start(f32[8,16,128]{2,1,0:T(8,128)} %sum_copies.2), calls=%async_computation.1 | async-start | bytes 131072 | tf_op jit(solution)/shard_map/all_to_all | solution.py:22
  62.0 37.6 %copy-start = (f32[2048,128]{1,0:T(8,128)S(1)}, f32[2048,128]{1,0:T(8,128)}, u32[]{:S(2)}) copy-start(f32[2048,128]{1,0:T(8,128)} %weights_ref.3) | copy-start | bytes 3145732
  70.0 23.6 %all-to-all-start.2 = ((f32[64,16,128]{2,1,0:T(8,128)}), f32[64,16,128]{2,1,0:T(8,128)S(1)}, u32[]{:S(2)}, u32[]{:S(2)}) async-start(f32[64,16,128]{2,1,0:T(8,128)} %sum_copies.3), calls=%async_computation.2 | async-start | bytes 1048576 | tf_op jit(solution)/shard_map/all_to_all | solution.py:22
  77.2 22.4 %copy-start.1 = (f32[2048]{0:T(1024)S(1)}, f32[2048]{0:T(1024)}, u32[]{:S(2)}) copy-start(f32[2048]{0:T(1024)} %param.17) | copy-start | bytes 24580
  77.2 16.4 %collective-permute-start.3 = (f32[2,4,64,128]{3,2,1,0:T(8,128)S(1)}, f32[2,4,64,128]{3,2,1,0:T(8,128)S(1)}, u32[]{:S(2)}, u32[]{:S(2)}) collective-permute-start(f32[2,4,64,128]{3,2,1,0:T(8,128)S(1)} %dynamic-slice_bitcast_fusion.1.ready_ref), channel_id=1, source_target_pairs={{0,64},{64,0},{1,65},{65,1},{2,66},{66,2},{3,67},{67,3},{4,68},{68... | collective-permute-start | bytes 786440 | tf_op jit(solution)/shard_map/ppermute | solution.py:46
  93.6 8.1 %collective-permute-start.4 = (f32[1024,128]{1,0:T(8,128)S(1)}, f32[1024,128]{1,0:T(8,128)S(1)}, u32[]{:S(2)}, u32[]{:S(2)}) collective-permute-start(f32[1024,128]{1,0:T(8,128)S(1)} %bitcast.26), channel_id=1, source_target_pairs={{0,16},{16,0},{1,17},{17,1},{2,18},{18,2},{3,19},{19,3},{4,20},{20... | collective-permute-start | bytes 1572872 | tf_op jit(solution)/shard_map/ppermute | solution.py:46

commit v7 on v6

--- a/solution.py
+++ b/solution.py
@@ -9,7 +9,7 @@
 SIZES = (2, 2, 2, 2, 2, 2, 2, 8)
 CODE = ("xh", "xm", "yh", "ym", "yl", "core")
 DP = ("xl", "z")
-NEAR = ("xh", "xm", "xl", "z")
+NEAR = ("z", "xh", "xm", "xl")
 TILE = 256
 FAR = ("yh", "ym", "yl")
 
@@ -216,8 +216,7 @@
     parts = exchange(grad.reshape(near, half // near, width), NEAR)
     parts = exchange(sum_copies(parts, size(FAR), send_near), FAR)
     grad = exchange(sum_copies(parts, near, send_far), NEAR).reshape(half, width)
-    grad, last = lax.optimization_barrier((grad, last))
-    parity_shards = (mine + last)[None, None]
+    grad, parity_shards = lax.optimization_barrier((grad, (mine + last)[None, None]))
     other = swap(grad, "core")
     sums = accum.reshape(hot_rows // width, width)
     done = adagrad_half(core, grad, hot_weights, sums)

time: 104 us -> 103 us (level)
  starting transfers between devices: 54 us -> 52.9 us
  transfers between devices with their start and end apart: 8 -> 8, of which waited for: 4 -> 5; matrix products, arithmetic and copies ran while one was open for 2% -> 2% of each run, Pallas kernels for 3% -> 3%
where the time goes in v7:
time: 103 us; the launch traced here: 102 us
  starting transfers between devices  52.9 us (51%)
  waiting for transfers between devices  33.9 us (33%)
  Pallas kernels  10.3 us (10%)
  other arithmetic  2.17 us (2%)
  between operations  2.11 us (2%)
  local copies, waits for them, and re-layouts  1.07 us (1%)
    ppermute x5, starting transfers between devices, swap(): return lax.ppermute(value, axis, [(0, 1), (1, 0)])  29.4 us
    all_to_all x3, starting transfers between devices, exchange(): return lax.all_to_all(parts, axes, 0, 0, tiled=True)  23.5 us
    all_to_all x3, waiting for transfers between devices, exchange(): return lax.all_to_all(parts, axes, 0, 0, tiled=True)  19.2 us
    ppermute x5, waiting for transfers between devices, swap(): return lax.ppermute(value, axis, [(0, 1), (1, 0)])  14.7 us
    pallas_call x1, Pallas kernels, front(): pl.pallas_call(front_kernel, out_shape=outs, in_specs=[scalar] * 5 + [who...  3.98 us
    pallas_call x2, Pallas kernels, adagrad_half(): pl.pallas_call(adagrad_kernel, grid_spec=pltpu.PrefetchScalarGridSpec(num...  2.61 us
  transfers between devices with their start and end apart: 8, of which 5 were waited for; matrix products, arithmetic and copies ran while one was open for 2% of the time, Pallas kernels for 3%

profile of v7, /device:TPU:1, one launch (start us, length us, event | category | flops | bytes accessed | tf_op | source)
XLA Modules:
  0.0 102.4 jit_solution(15389554672005066807)
XLA Ops:
  1.9 0.0 copy-start.2
  1.9 0.0 copy-start.3
  1.9 4.0 %front.1 = (f32[1024,128]{1,0:T(8,128)}, f32[2,4,4,64,128]{4,3,2,1,0:T(8,128)}, f32[2,4,4,64,128]{4,3,2,1,0:T(8,128)}) custom-call(s32[1]{0:T(128)} %bitcast.core_ref.place_ref, s32[1,1,4]{2,1,0:T(1,128)} %blocks_ref.1, s32[1,1]{1,0:T(1,128)S(6)} %copy.20.counts_ref, s32[1]{0:T(128)S(6)} %copy.21.column_ref, f32[2,8]{1,0:T(2,128)} %coef_ref.1, ...), custom_call_target="tpu_custom_call" | custom-call | flops 805306368 | bytes 4194304 | tf_op jit(solution)/shard_map/front/pallas_call | solution.py:141
  5.9 16.1 %collective-permute-start = (f32[1024,128]{1,0:T(8,128)}, f32[1024,128]{1,0:T(8,128)S(1)}, u32[]{:S(2)}, u32[]{:S(2)}) collective-permute-start(f32[1024,128]{1,0:T(8,128)} %get-tuple-element.15), channel_id=1, source_target_pairs={{0,16},{16,0},{1,17},{17,1},{2,18},{18,2},{3,19},{19,3},{4,20},{20... | collective-permute-start | bytes 1572872 | tf_op jit(solution)/shard_map/ppermute | solution.py:46
  22.0 1.3 %hot_rows_sum.1.left_ref = f32[1024,128]{1,0:T(8,128)S(1)} custom-call(s32[1]{0:T(128)} %bitcast.core_ref.place_ref, s32[1,1024]{1,0:T(1,128)S(1)} %bitcast.33, f32[1024,128]{1,0:T(8,128)S(1)} %bitcast.31), custom_call_target="tpu_custom_call" | custom-call | flops 805306368 | bytes 1048576 | tf_op jit(solution)/shard_map/hot_rows_sum/pallas_call | solution.py:95
  23.3 0.0 copy-start.4
  23.3 0.4 collective-permute-done.right_ref
  23.7 0.9 added.1
  24.6 2.3 %collective-permute-start.1 = (f32[2,4,4,64,128]{4,3,2,1,0:T(8,128)}, f32[2,4,4,64,128]{4,3,2,1,0:T(8,128)S(1)}, u32[]{:S(2)}, u32[]{:S(2)}) collective-permute-start(f32[2,4,4,64,128]{4,3,2,1,0:T(8,128)} %get-tuple-element.18), channel_id=1, source_target_pairs={{0,16},{16,0},{1,17},{17,1},{2,18},{18,2},{3,19},{19,3},{4,20},{20... | collective-permute-start | bytes 3145736 | tf_op jit(solution)/shard_map/ppermute | solution.py:46
  26.9 9.7 %all-to-all-start = ((f32[64,16,128]{2,1,0:T(8,128)}), f32[64,16,128]{2,1,0:T(8,128)S(1)}, u32[]{:S(2)}, u32[]{:S(2)}) async-start(f32[64,16,128]{2,1,0:T(8,128)} %bitcast.4), calls=%async_computation | async-start | bytes 1048576 | tf_op jit(solution)/shard_map/all_to_all | solution.py:22
  36.6 0.0 collective-permute-done.1
  36.6 1.0 copy-done.5
  37.6 0.0 copy-done.4
  37.6 1.4 %add.25 = f32[2,4,4,64,128]{4,3,2,1,0:T(8,128)S(1)} add(f32[2,4,4,64,128]{4,3,2,1,0:T(8,128)S(1)} %copy-done.4, f32[2,4,4,64,128]{4,3,2,1,0:T(8,128)} %copy-done.5) | non-fusion elementwise | flops 262144 | bytes 3145728 | tf_op jit(solution)/shard_map/add | solution.py:207
  38.9 0.1 dynamic-slice_bitcast_fusion.ready_ref
  39.0 3.3 %collective-permute-start.2 = (f32[2,4,2,64,128]{4,3,2,1,0:T(8,128)S(1)}, f32[2,4,2,64,128]{4,3,2,1,0:T(8,128)S(1)}, u32[]{:S(2)}, u32[]{:S(2)}) collective-permute-start(f32[2,4,2,64,128]{4,3,2,1,0:T(8,128)S(1)} %dynamic-slice_bitcast_fusion.ready_ref), channel_id=1, source_target_pairs={{0,32},{32,0},{1,33},{33,1},{2,34},{34,2},{3,35},{35,3},{4,36},{36... | collective-permute-start | bytes 1572872 | tf_op jit(solution)/shard_map/ppermute | solution.py:46
  42.3 12.1 %all-to-all-done.parts_ref = f32[64,16,128]{2,1,0:T(8,128)S(1)} async-done(((f32[64,16,128]{2,1,0:T(8,128)}), f32[64,16,128]{2,1,0:T(8,128)S(1)}, u32[]{:S(2)}, u32[]{:S(2)}) %all-to-all-start) | async-done | bytes 524320 | tf_op jit(solution)/shard_map/all_to_all | solution.py:22
  54.4 0.7 sum_copies.2
  55.2 7.3 %all-to-all-start.1 = ((f32[8,16,128]{2,1,0:T(8,128)}), f32[8,16,128]{2,1,0:T(8,128)S(1)}, u32[]{:S(2)}, u32[]{:S(2)}) async-start(f32[8,16,128]{2,1,0:T(8,128)} %sum_copies.2), calls=%async_computation.1 | async-start | bytes 131072 | tf_op jit(solution)/shard_map/all_to_all | solution.py:22
  62.4 0.0 collective-permute-done.2
  62.4 0.1 bitcast_add_fusion
  62.6 7.1 %all-to-all-done.1.parts_ref = f32[8,16,128]{2,1,0:T(8,128)S(1)} async-done(((f32[8,16,128]{2,1,0:T(8,128)}), f32[8,16,128]{2,1,0:T(8,128)S(1)}, u32[]{:S(2)}, u32[]{:S(2)}) %all-to-all-start.1) | async-done | bytes 65568 | tf_op jit(solution)/shard_map/all_to_all | solution.py:22
  69.7 0.8 sum_copies.3
  70.5 6.5 %all-to-all-start.2 = ((f32[64,16,128]{2,1,0:T(8,128)}), f32[64,16,128]{2,1,0:T(8,128)S(1)}, u32[]{:S(2)}, u32[]{:S(2)}) async-start(f32[64,16,128]{2,1,0:T(8,128)} %sum_copies.3), calls=%async_computation.2 | async-start | bytes 1048576 | tf_op jit(solution)/shard_map/all_to_all | solution.py:22
  77.0 2.1 %collective-permute-start.3 = (f32[2,4,64,128]{3,2,1,0:T(8,128)S(1)}, f32[2,4,64,128]{3,2,1,0:T(8,128)S(1)}, u32[]{:S(2)}, u32[]{:S(2)}) collective-permute-start(f32[2,4,64,128]{3,2,1,0:T(8,128)S(1)} %dynamic-slice_bitcast_fusion.1.ready_ref), channel_id=1, source_target_pairs={{0,64},{64,0},{1,65},{65,1},{2,66},{66,2},{3,67},{67,3},{4,68},{68... | collective-permute-start | bytes 786440 | tf_op jit(solution)/shard_map/ppermute | solution.py:46
  79.1 14.0 %collective-permute-done.3 = f32[2,4,64,128]{3,2,1,0:T(8,128)S(1)} collective-permute-done((f32[2,4,64,128]{3,2,1,0:T(8,128)S(1)}, f32[2,4,64,128]{3,2,1,0:T(8,128)S(1)}, u32[]{:S(2)}, u32[]{:S(2)}) %collective-permute-start.3) | collective-permute-done | bytes 262176 | tf_op jit(solution)/shard_map/ppermute | solution.py:46
  93.2 0.7 fusion
  93.9 0.0 all-to-all-done.2
  93.9 5.6 %collective-permute-start.4 = (f32[1024,128]{1,0:T(8,128)S(1)}, f32[1024,128]{1,0:T(8,128)S(1)}, u32[]{:S(2)}, u32[]{:S(2)}) collective-permute-start(f32[1024,128]{1,0:T(8,128)S(1)} %bitcast.26), channel_id=1, source_target_pairs={{0,16},{16,0},{1,17},{17,1},{2,18},{18,2},{3,19},{19,3},{4,20},{20... | collective-permute-start | bytes 1572872 | tf_op jit(solution)/shard_map/ppermute | solution.py:46
  99.6 1.3 %hot_rows_adagrad.2 = (f32[2048,128]{1,0:T(8,128)}, f32[16,128]{1,0:T(8,128)}) custom-call(s32[1]{0:T(128)} %bitcast.core_ref.place_ref, f32[1024,128]{1,0:T(8,128)S(1)} %bitcast.27, f32[2048,128]{1,0:T(8,128)S(1)} %copy-done, f32[16,128]{1,0:T(8,128)S(1)} %bitcast.28), custom_call_target="tpu_custom_call" | custom-call | flops 1048576 | bytes 1572864 | tf_op jit(solution)/shard_map/hot_rows_adagrad/pallas_call | solution.py:171
  100.9 0.2 collective-permute-done.4.grad_ref
  101.1 1.3 %hot_rows_adagrad.3 = (f32[2048,128]{1,0:T(8,128)}, f32[16,128]{1,0:T(8,128)}) custom-call(s32[1]{0:T(128)} %bitcast.12.place_ref, f32[1024,128]{1,0:T(8,128)S(1)} %collective-permute-done.4.grad_ref, f32[2048,128]{1,0:T(8,128)S(1)} %copy-done, f32[16,128]{1,0:T(8,128)S(1)} %bitcast.29, ...), custom_call_target="tpu_custom_call", output_to_operand_aliasing={{0}: (4, {}), {1}: (5, {})} | custom-call | flops 1048576 | bytes 1572864 | tf_op jit(solution)/shard_map/hot_rows_adagrad/pallas_call | solution.py:171
  (8 shorter events, 0.0 us)
Async XLA Ops:
  1.9 20.1 %copy-start.2 = (f32[1,1,1024,128]{3,2,1,0:T(8,128)S(1)}, f32[1,1,1024,128]{3,2,1,0:T(8,128)}, u32[]{:S(2)}) copy-start(f32[1,1,1024,128]{3,2,1,0:T(8,128)} %param.15) | copy-start | bytes 1572868
  1.9 20.1 %copy-start.3 = (s32[1,1,1024]{2,1,0:T(1,128)S(1)}, s32[1,1,1024]{2,1,0:T(1,128)}, u32[]{:S(2)}) copy-start(s32[1,1,1024]{2,1,0:T(1,128)} %param.14) | copy-start | bytes 12292
  5.9 17.8 %collective-permute-start = (f32[1024,128]{1,0:T(8,128)}, f32[1024,128]{1,0:T(8,128)S(1)}, u32[]{:S(2)}, u32[]{:S(2)}) collective-permute-start(f32[1024,128]{1,0:T(8,128)} %get-tuple-element.15), channel_id=1, source_target_pairs={{0,16},{16,0},{1,17},{17,1},{2,18},{18,2},{3,19},{19,3},{4,20},{20... | collective-permute-start | bytes 1572872 | tf_op jit(solution)/shard_map/ppermute | solution.py:46
  23.3 14.3 %copy-start.4 = (f32[2,4,4,64,128]{4,3,2,1,0:T(8,128)S(1)}, f32[2,4,4,64,128]{4,3,2,1,0:T(8,128)}, u32[]{:S(2)}) copy-start(f32[2,4,4,64,128]{4,3,2,1,0:T(8,128)} %get-tuple-element.17) | copy-start | bytes 3145732
  24.6 12.0 %collective-permute-start.1 = (f32[2,4,4,64,128]{4,3,2,1,0:T(8,128)}, f32[2,4,4,64,128]{4,3,2,1,0:T(8,128)S(1)}, u32[]{:S(2)}, u32[]{:S(2)}) collective-permute-start(f32[2,4,4,64,128]{4,3,2,1,0:T(8,128)} %get-tuple-element.18), channel_id=1, source_target_pairs={{0,16},{16,0},{1,17},{17,1},{2,18},{18,2},{3,19},{19,3},{4,20},{20... | collective-permute-start | bytes 3145736 | tf_op jit(solution)/shard_map/ppermute | solution.py:46
  26.9 27.6 %all-to-all-start = ((f32[64,16,128]{2,1,0:T(8,128)}), f32[64,16,128]{2,1,0:T(8,128)S(1)}, u32[]{:S(2)}, u32[]{:S(2)}) async-start(f32[64,16,128]{2,1,0:T(8,128)} %bitcast.4), calls=%async_computation | async-start | bytes 1048576 | tf_op jit(solution)/shard_map/all_to_all | solution.py:22
  36.6 1.0 copy-start.5
  39.0 23.4 %collective-permute-start.2 = (f32[2,4,2,64,128]{4,3,2,1,0:T(8,128)S(1)}, f32[2,4,2,64,128]{4,3,2,1,0:T(8,128)S(1)}, u32[]{:S(2)}, u32[]{:S(2)}) collective-permute-start(f32[2,4,2,64,128]{4,3,2,1,0:T(8,128)S(1)} %dynamic-slice_bitcast_fusion.ready_ref), channel_id=1, source_target_pairs={{0,32},{32,0},{1,33},{33,1},{2,34},{34,2},{3,35},{35,3},{4,36},{36... | collective-permute-start | bytes 1572872 | tf_op jit(solution)/shard_map/ppermute | solution.py:46
  55.2 14.5 %all-to-all-start.1 = ((f32[8,16,128]{2,1,0:T(8,128)}), f32[8,16,128]{2,1,0:T(8,128)S(1)}, u32[]{:S(2)}, u32[]{:S(2)}) async-start(f32[8,16,128]{2,1,0:T(8,128)} %sum_copies.2), calls=%async_computation.1 | async-start | bytes 131072 | tf_op jit(solution)/shard_map/all_to_all | solution.py:22
  70.5 29.1 %copy-start = (f32[2048,128]{1,0:T(8,128)S(1)}, f32[2048,128]{1,0:T(8,128)}, u32[]{:S(2)}) copy-start(f32[2048,128]{1,0:T(8,128)} %weights_ref.3) | copy-start | bytes 3145732
  70.5 23.4 %all-to-all-start.2 = ((f32[64,16,128]{2,1,0:T(8,128)}), f32[64,16,128]{2,1,0:T(8,128)S(1)}, u32[]{:S(2)}, u32[]{:S(2)}) async-start(f32[64,16,128]{2,1,0:T(8,128)} %sum_copies.3), calls=%async_computation.2 | async-start | bytes 1048576 | tf_op jit(solution)/shard_map/all_to_all | solution.py:22
  77.0 16.2 %collective-permute-start.3 = (f32[2,4,64,128]{3,2,1,0:T(8,128)S(1)}, f32[2,4,64,128]{3,2,1,0:T(8,128)S(1)}, u32[]{:S(2)}, u32[]{:S(2)}) collective-permute-start(f32[2,4,64,128]{3,2,1,0:T(8,128)S(1)} %dynamic-slice_bitcast_fusion.1.ready_ref), channel_id=1, source_target_pairs={{0,64},{64,0},{1,65},{65,1},{2,66},{66,2},{3,67},{67,3},{4,68},{68... | collective-permute-start | bytes 786440 | tf_op jit(solution)/shard_map/ppermute | solution.py:46
  93.2 6.4 %copy-start.1 = (f32[2048]{0:T(1024)S(1)}, f32[2048]{0:T(1024)}, u32[]{:S(2)}) copy-start(f32[2048]{0:T(1024)} %param.17) | copy-start | bytes 24580
  93.9 7.2 %collective-permute-start.4 = (f32[1024,128]{1,0:T(8,128)S(1)}, f32[1024,128]{1,0:T(8,128)S(1)}, u32[]{:S(2)}, u32[]{:S(2)}) collective-permute-start(f32[1024,128]{1,0:T(8,128)S(1)} %bitcast.26), channel_id=1, source_target_pairs={{0,16},{16,0},{1,17},{17,1},{2,18},{18,2},{3,19},{19,3},{4,20},{20... | collective-permute-start | bytes 1572872 | tf_op jit(solution)/shard_map/ppermute | solution.py:46
